TPU v7x, 32 devices: a whole 2x2x4 slice. The times are simulated.
32 devices in a mesh: sect: 4 (over x, core), lat: 2 (over y), var: 4 (over z).
Axes of the slice: x: 2, y: 2, z: 4, core: 2. Of those that a mesh axis runs over, the one named last changes fastest.
Arguments:
- patches: bfloat16 [16, 16, 256, 128], P(('sect', 'var'), 'lat'), may hold values from -6 to 6
- embed_weight: bfloat16 [16, 128, 512], P(('sect', 'var')), may hold values from -0.1875 to 0.1875
- qkv_weight: bfloat16 [2, 512, 3, 512], P(None, None, None, 'var'), may hold values from -0.25 to 0.25
- out_weight: bfloat16 [2, 512, 512], P(None, 'var'), may hold values from -2 to 2
- mlp_in_weight: bfloat16 [2, 512, 2048], P(None, None, 'var'), may hold values from -0.25 to 0.25
- mlp_out_weight: bfloat16 [2, 2048, 512], P(None, 'var'), may hold values from -2 to 2
- logit_scale: float32 [2, 8], P(None, 'var'), may hold values from 3 to 30
- norm_gain: float32 [2, 2, 512], P(None, None, 'var'), may hold values from 0.1 to 1.9
- norm_bias: float32 [2, 2, 512], P(None, None, 'var'), may hold values from -2.5 to 2.5
- decode_weight: bfloat16 [16, 512, 128], P(('sect', 'var')), may hold values from -0.25 to 0.25
- shifts: int32 [2, 2], replicated, may hold values from 1 to 7
Outputs:
- decoded: bfloat16 [16, 16, 256, 128], P(('sect', 'var'), 'lat')
All inputs are finite; a program needn't handle non-finite values.
Results may differ from a plain program's by a relative error of at most 0.034.
Values may be sent and summed in bfloat16 or wider, within the bound.
A program may use at most 128 MiB of HBM per device.

v0:
```python
import jax
import jax.numpy as jnp
from jax import lax
from jax.sharding import PartitionSpec as P

WL = 8
WW = 16


epsilon = 1e-06


def extended(array, sides, width, wrap):
    for axis, dim in sides:
        size, length = (lax.axis_size(axis), array.shape[dim])
        up = [(i, (i + 1) % size) for i in range(size if wrap else size - 1)]
        down = [(j, i) for i, j in up]
        last = lax.slice_in_dim(array, length - width, length, axis=dim)
        initial = lax.slice_in_dim(array, 0, width, axis=dim)
        before = lax.ppermute(last, axis, up)
        after = lax.ppermute(initial, axis, down)
        array = jnp.concatenate([before, array, after], axis=dim)
    return array


def unit_norm(vector_rows, heads_local, head_dim):
    shaped = vector_rows.reshape(vector_rows.shape[0], vector_rows.shape[1], heads_local, head_dim)
    shaped = shaped * lax.rsqrt(jnp.sum(shaped * shaped, axis=-1, keepdims=True) + epsilon)
    return shaped.reshape(vector_rows.shape).astype(jnp.bfloat16)


def to_windows(frame, win_rows, win_cols, heads_local, head_dim):
    shaped = frame.reshape(win_rows, WL, win_cols, WW, heads_local, head_dim)
    return shaped.transpose(0, 2, 1, 3, 4, 5).reshape(
        win_rows, win_cols, WL * WW, heads_local, head_dim
    )


def post_norm(stream, mixed_sum, sums, squares, model_width, gain_row, bias_row):
    avg_feat = sums[:, :, None] / model_width
    variance = squares[:, :, None] / model_width - avg_feat * avg_feat
    normed = (mixed_sum - avg_feat) * lax.rsqrt(variance + 1e-05)
    return (stream.astype(jnp.float32) + gain_row * normed + bias_row).astype(jnp.bfloat16)


def project(gathered, wqkv, heads_local, head_dim):
    projected = jnp.einsum("rld,dce->rlce", gathered, wqkv, preferred_element_type=jnp.float32)
    queries = unit_norm(projected[:, :, 0], heads_local, head_dim)
    key_vals = unit_norm(projected[:, :, 1], heads_local, head_dim)
    values = projected[:, :, 2].astype(jnp.bfloat16)
    return (queries, jnp.stack([key_vals, values], axis=2))


def attend(queries, paired, head_scale, shift_lat, shift_lon, heads_local, head_dim):
    lat_rows, lon_cols, head_cols = queries.shape
    query_pad = jnp.pad(queries, ((WL, WL), (WW, WW), (0, 0)))
    frame_rows = lat_rows + WL
    frame_cols = lon_cols + WW
    win_rows = frame_rows // WL
    win_cols = frame_cols // WW
    q_frame = lax.dynamic_slice(
        query_pad, (shift_lat, shift_lon, 0), (frame_rows, frame_cols, head_cols)
    )
    kv_frame = lax.dynamic_slice(
        paired, (shift_lat, shift_lon, 0, 0), (frame_rows, frame_cols, 2, head_cols)
    )
    q_win = to_windows(q_frame, win_rows, win_cols, heads_local, head_dim)
    k_win = to_windows(kv_frame[:, :, 0], win_rows, win_cols, heads_local, head_dim)
    v_win = to_windows(kv_frame[:, :, 1], win_rows, win_cols, heads_local, head_dim)
    scores = (
        jnp.einsum("wnqhe,wnkhe->wnhqk", q_win, k_win, preferred_element_type=jnp.float32)
        * head_scale[:, None, None]
    )
    lat_total = lat_rows * lax.axis_size("lat")
    global_row = (
        lax.axis_index("lat") * lat_rows - WL + shift_lat + jnp.arange(frame_rows, dtype=jnp.int32)
    )
    usable = (global_row >= 0) & (global_row < lat_total)
    usable = jnp.broadcast_to(
        usable.reshape(win_rows, 1, WL, 1), (win_rows, win_cols, WL, WW)
    ).reshape(win_rows, win_cols, 1, 1, WL * WW)
    scores = jnp.where(usable, scores, -1e30)
    top = jnp.max(scores, axis=-1, keepdims=True)
    expo = jnp.exp(scores - top)
    weights = (expo / jnp.sum(expo, axis=-1, keepdims=True)).astype(jnp.bfloat16)
    attended = jnp.einsum(
        "wnhqk,wnkhe->wnqhe", weights, v_win, preferred_element_type=jnp.float32
    ).astype(jnp.bfloat16)
    attended = (
        attended.reshape(win_rows, win_cols, WL, WW, head_cols)
        .transpose(0, 2, 1, 3, 4)
        .reshape(frame_rows, frame_cols, head_cols)
    )
    return lax.dynamic_slice(
        attended, (WL - shift_lat, WW - shift_lon, 0), (lat_rows, lon_cols, head_cols)
    )


def layer_heads(stream, wqkv, wout, w_in, w_out, head_scale, gains, biases, shift_lat, shift_lon):
    heads_local = head_scale.shape[0]
    head_dim = wqkv.shape[2] // heads_local
    gathered = lax.all_gather(stream, "var", axis=2, tiled=True)
    model_width = gathered.shape[2]
    queries, paired = project(gathered, wqkv, heads_local, head_dim)
    paired = extended(paired, (("lat", 0),), WL, False)
    paired = extended(paired, (("sect", 1),), WW, True)
    own_rows = attend(queries, paired, head_scale, shift_lat, shift_lon, heads_local, head_dim)
    partial_value = jnp.einsum("rle,ed->rld", own_rows, wout, preferred_element_type=jnp.float32)
    mixed_sum = lax.psum_scatter(partial_value, "var", scatter_dimension=2, tiled=True)
    totals = lax.psum((jnp.sum(mixed_sum, axis=-1), jnp.sum(mixed_sum * mixed_sum, axis=-1)), "var")
    attn_stream = post_norm(
        stream, mixed_sum, totals[0], totals[1], model_width, gains[0], biases[0]
    )
    widened = lax.all_gather(attn_stream, "var", axis=2, tiled=True)
    hidden = jax.nn.gelu(
        jnp.einsum("rld,df->rlf", widened, w_in, preferred_element_type=jnp.float32)
    ).astype(jnp.bfloat16)
    part_fed = jnp.einsum("rlf,fd->rld", hidden, w_out, preferred_element_type=jnp.float32)
    fed = lax.psum_scatter(part_fed, "var", scatter_dimension=2, tiled=True)
    fed_totals = lax.psum((jnp.sum(fed, axis=-1), jnp.sum(fed * fed, axis=-1)), "var")
    return post_norm(
        attn_stream, fed, fed_totals[0], fed_totals[1], model_width, gains[1], biases[1]
    )


def per_device(
    patches,
    embed_weight,
    qkv_weight,
    out_weight,
    mlp_in_weight,
    mlp_out_weight,
    logit_scale,
    norm_gain,
    norm_bias,
    decode_weight,
    shifts,
):
    groups, lat_rows, lon_total, patch_dim = patches.shape
    model_width = embed_weight.shape[2]
    sect_count = lax.axis_size("sect")
    var_count = lax.axis_size("var")
    lon_cols = lon_total // sect_count
    feat_part = model_width // var_count
    blocks = patches.reshape(groups, lat_rows, sect_count, lon_cols, patch_dim)
    tables = embed_weight.reshape(groups, patch_dim, var_count, feat_part)
    partial_value = jnp.einsum(
        "vrclp,vpkd->rckld", blocks, tables, preferred_element_type=jnp.float32
    )
    partial_value = partial_value.reshape(lat_rows, sect_count * var_count * lon_cols, feat_part)
    stream = lax.psum_scatter(
        partial_value, ("sect", "var"), scatter_dimension=1, tiled=True
    ).astype(jnp.bfloat16)
    for layer_id in range(qkv_weight.shape[0]):
        stream = layer_heads(
            stream,
            qkv_weight[layer_id],
            out_weight[layer_id],
            mlp_in_weight[layer_id],
            mlp_out_weight[layer_id],
            logit_scale[layer_id],
            norm_gain[layer_id],
            norm_bias[layer_id],
            shifts[layer_id, 0],
            shifts[layer_id, 1],
        )
    gathered = lax.all_gather(stream, "var", axis=2, tiled=True)
    return jnp.einsum(
        "rld,vdp->vrlp",
        lax.all_gather(gathered, "sect", axis=1, tiled=True),
        decode_weight,
        preferred_element_type=jnp.float32,
    ).astype(jnp.bfloat16)


def solution(mesh):
    return jax.shard_map(
        per_device,
        mesh=mesh,
        in_specs=(
            P(("sect", "var"), "lat", None, None),
            P(("sect", "var"), None, None),
            P(None, None, None, "var"),
            P(None, "var", None),
            P(None, None, "var"),
            P(None, "var", None),
            P(None, "var"),
            P(None, None, "var"),
            P(None, None, "var"),
            P(("sect", "var"), None, None),
            P(),
        ),
        out_specs=P(("sect", "var"), "lat", None, None),
        check_vma=False,
    )
```

profile of v0, /device:TPU:0, one launch (start us, length us, event | category | flops | bytes accessed | tf_op | source)
XLA Modules:
  0.0 410.9 jit_solution(1697369271195773828)
XLA Ops:
  6.5 1.0 reshape.174
  7.6 0.7 convolution_bitcast_fusion
  8.3 2.2 copy.22
  10.7 0.6 copy-done.7
  11.3 0.6 fusion.97
  13.2 73.2 %reduce-scatter.6.cloned.1.call-done = f32[8,64,128]{2,1,0:T(8,128)} async-done(((f32[8,1024,128]{2,1,0:T(8,128)}), f32[8,64,128]{2,1,0:T(8,128)}) %reduce-scatter.6.cloned.1.call-update) | async-done | bytes 262160 | tf_op jit(solution)/shard_map/reduce_scatter | solution.py:151
  86.4 1.0 convert_element_type.84
  87.3 14.7 %all_gather.18 = bf16[8,64,512]{2,1,0:T(8,128)(2,1)S(1)} all-gather(bf16[8,64,128]{2,1,0:T(8,128)(2,1)S(1)} %convert_element_type.84), channel_id=1, replica_groups=mesh['sect'=4,'lat'=2,'var'=4] {'var'}, dimensions={2}, use_global_device_ids=true | all-gather | bytes 655360 | tf_op jit(solution)/shard_map/all_gather | solution.py:102
  102.9 0.6 reduce_sum.126
  103.6 0.6 mul.238
  104.6 3.2 collective-permute-start
  107.8 1.3 collective-permute-start.1
  116.0 0.6 reduce_sum.127
  116.7 0.6 mul.244
  117.6 0.7 pad_maximum_fusion.6
  118.3 1.7 collective-permute-start.3
  121.0 3.3 collective-permute-done.2
  124.6 1.5 fusion.35
  126.1 0.8 fusion.96
  127.3 0.6 fusion.7
  127.9 0.7 fusion.98
  128.5 1.3 reshape_squeeze.20
  131.5 1.3 fusion.72
  132.9 27.5 %reduce-scatter.8.cloned.1.call-done = f32[8,64,128]{2,1,0:T(8,128)} async-done(((f32[8,64,512]{2,1,0:T(8,128)}), f32[8,64,128]{2,1,0:T(8,128)}) %reduce-scatter.8.cloned.1.call-update) | async-done | bytes 262160 | tf_op jit(solution)/shard_map/reduce_scatter | solution.py:109
  160.3 1.2 fusion.94
  161.5 9.6 %all-reduce.5 = (f32[8,64]{1,0:T(8,128)S(1)}, f32[8,64]{1,0:T(8,128)S(1)}) all-reduce(f32[8,64]{1,0:T(8,128)S(1)} %get-tuple-element.12, f32[8,64]{1,0:T(8,128)S(1)} %get-tuple-element.11), channel_id=1, replica_groups=mesh['sect'=4,'lat'=2,'var'=4] {'var'}, use_global_device_ids=true, to_apply=%region_9.10 | all-reduce | flops 1024 | bytes 8192 | tf_op jit(solution)/shard_map/psum | solution.py:110
  171.1 1.2 add_convert_fusion.3
  172.3 14.0 %all_gather.19 = bf16[8,64,512]{2,1,0:T(8,128)(2,1)S(1)} all-gather(bf16[8,64,128]{2,1,0:T(8,128)(2,1)S(1)} %add_convert_fusion.3), channel_id=1, replica_groups=mesh['sect'=4,'lat'=2,'var'=4] {'var'}, dimensions={2}, use_global_device_ids=true | all-gather | bytes 655360 | tf_op jit(solution)/shard_map/all_gather | solution.py:114
  186.3 1.9 fusion.19
  188.2 26.1 %reduce-scatter.10.cloned.1.call-done = f32[8,64,128]{2,1,0:T(8,128)} async-done(((f32[8,64,512]{2,1,0:T(8,128)}), f32[8,64,128]{2,1,0:T(8,128)}) %reduce-scatter.10.cloned.1.call-update) | async-done | bytes 262160 | tf_op jit(solution)/shard_map/reduce_scatter | solution.py:119
  214.4 1.2 fusion.93
  215.5 9.5 %all-reduce.4 = (f32[8,64]{1,0:T(8,128)S(1)}, f32[8,64]{1,0:T(8,128)S(1)}) all-reduce(f32[8,64]{1,0:T(8,128)S(1)} %get-tuple-element.10, f32[8,64]{1,0:T(8,128)S(1)} %get-tuple-element.9), channel_id=1, replica_groups=mesh['sect'=4,'lat'=2,'var'=4] {'var'}, use_global_device_ids=true, to_apply=%region_14.15 | all-reduce | flops 1024 | bytes 8192 | tf_op jit(solution)/shard_map/psum | solution.py:120
  225.1 1.2 add_convert_fusion.2
  226.3 13.8 %all_gather.20 = bf16[8,64,512]{2,1,0:T(8,128)(2,1)S(1)} all-gather(bf16[8,64,128]{2,1,0:T(8,128)(2,1)S(1)} %add_convert_fusion.2), channel_id=1, replica_groups=mesh['sect'=4,'lat'=2,'var'=4] {'var'}, dimensions={2}, use_global_device_ids=true | all-gather | bytes 655360 | tf_op jit(solution)/shard_map/all_gather | solution.py:102
  240.9 0.6 reduce_sum.133
  241.6 0.6 mul.270
  242.6 3.4 collective-permute-start.4
  246.1 1.3 collective-permute-start.5
  254.2 0.6 reduce_sum.134
  254.9 0.6 mul.275
  255.8 0.8 pad_maximum_fusion.2
  256.6 1.7 collective-permute-start.7
  259.2 3.0 collective-permute-done.6
  262.1 0.9 collective-permute-done.7
  263.1 1.5 fusion.30
  264.5 0.8 fusion.95
  265.7 0.6 fusion.6
  266.3 0.7 fusion.99
  267.0 1.3 reshape_squeeze.23
  268.4 0.6 fusion.10
  269.9 1.3 fusion.70
  271.3 27.7 %reduce-scatter.12.cloned.1.call-done = f32[8,64,128]{2,1,0:T(8,128)} async-done(((f32[8,64,512]{2,1,0:T(8,128)}), f32[8,64,128]{2,1,0:T(8,128)}) %reduce-scatter.12.cloned.1.call-update) | async-done | bytes 262160 | tf_op jit(solution)/shard_map/reduce_scatter | solution.py:109
  298.9 1.2 fusion.92
  300.1 9.5 %all-reduce.3 = (f32[8,64]{1,0:T(8,128)S(1)}, f32[8,64]{1,0:T(8,128)S(1)}) all-reduce(f32[8,64]{1,0:T(8,128)S(1)} %get-tuple-element.8, f32[8,64]{1,0:T(8,128)S(1)} %get-tuple-element.7), channel_id=1, replica_groups=mesh['sect'=4,'lat'=2,'var'=4] {'var'}, use_global_device_ids=true, to_apply=%region_23.24 | all-reduce | flops 1024 | bytes 8192 | tf_op jit(solution)/shard_map/psum | solution.py:110
  309.7 1.2 add_convert_fusion.1
  310.8 13.8 %all_gather.21 = bf16[8,64,512]{2,1,0:T(8,128)(2,1)S(1)} all-gather(bf16[8,64,128]{2,1,0:T(8,128)(2,1)S(1)} %add_convert_fusion.1), channel_id=1, replica_groups=mesh['sect'=4,'lat'=2,'var'=4] {'var'}, dimensions={2}, use_global_device_ids=true | all-gather | bytes 655360 | tf_op jit(solution)/shard_map/all_gather | solution.py:114
  324.7 1.9 fusion.28
  326.6 26.1 %reduce-scatter.14.cloned.1.call-done = f32[8,64,128]{2,1,0:T(8,128)} async-done(((f32[8,64,512]{2,1,0:T(8,128)}), f32[8,64,128]{2,1,0:T(8,128)}) %reduce-scatter.14.cloned.1.call-update) | async-done | bytes 262160 | tf_op jit(solution)/shard_map/reduce_scatter | solution.py:119
  352.8 1.2 fusion.91
  353.9 9.5 %all-reduce.2 = (f32[8,64]{1,0:T(8,128)S(1)}, f32[8,64]{1,0:T(8,128)S(1)}) all-reduce(f32[8,64]{1,0:T(8,128)S(1)} %get-tuple-element.6, f32[8,64]{1,0:T(8,128)S(1)} %get-tuple-element.5), channel_id=1, replica_groups=mesh['sect'=4,'lat'=2,'var'=4] {'var'}, use_global_device_ids=true, to_apply=%region_28.29 | all-reduce | flops 1024 | bytes 8192 | tf_op jit(solution)/shard_map/psum | solution.py:120
  363.5 1.2 add_convert_fusion
  364.6 14.5 %all_gather.22 = bf16[8,64,512]{2,1,0:T(8,128)(2,1)} all-gather(bf16[8,64,128]{2,1,0:T(8,128)(2,1)S(1)} %add_convert_fusion), channel_id=1, replica_groups=mesh['sect'=4,'lat'=2,'var'=4] {'var'}, dimensions={2}, use_global_device_ids=true | all-gather | bytes 655360 | tf_op jit(solution)/shard_map/all_gather | solution.py:167
  379.1 21.8 %all-gather.2.cloned.1.call-done = bf16[8,256,512]{2,1,0:T(8,128)(2,1)} async-done(((bf16[8,64,512]{2,1,0:T(8,128)(2,1)}), bf16[8,256,512]{2,1,0:T(8,128)(2,1)}) %all-gather.2.cloned.1.call-update) | async-done | bytes 2097168 | tf_op jit(solution)/shard_map/all_gather | solution.py:170
  401.0 3.1 fusion.8
  (102 shorter events, 10.2 us)
Async XLA Ops:
  6.5 1.1 copy-start
  6.5 79.8 %reduce-scatter.6.cloned.1.call-start = ((), (), s32[]{:S(2)}) async-start(), calls=%async_computation.5 | async-start | bytes 4456448 | tf_op jit(solution)/shard_map/reduce_scatter | solution.py:151
  10.6 0.7 copy-start.7
  10.6 2.6 copy-start.10
  10.6 91.5 %copy-start.2 = (bf16[2,512,3,128]{3,1,2,0:T(8,128)(2,1)S(1)}, bf16[2,512,3,128]{3,1,2,0:T(8,128)(2,1)}, u32[]{:S(2)}) copy-start(bf16[2,512,3,128]{3,1,2,0:T(8,128)(2,1)} %param.13) | copy-start | bytes 2359300
  10.6 149.7 %reduce-scatter.8.cloned.1.call-start = ((), (), s32[]{:S(2)}) async-start(), calls=%async_computation.6 | async-start | bytes 1310720 | tf_op jit(solution)/shard_map/reduce_scatter | solution.py:109
  104.6 13.0 %collective-permute-start = (bf16[8,64,2,128]{3,1,2,0:T(8,128)(2,1)S(1)}, bf16[8,64,2,128]{3,1,2,0:T(8,128)(2,1)S(1)}, u32[]{:S(2)}, u32[]{:S(2)}) collective-permute-start(bf16[8,64,2,128]{3,1,2,0:T(8,128)(2,1)S(1)} %pad_maximum_fusion), channel_id=1, source_target_pairs={{0,4},{1,5},{2,6},{3,7},{8,12},{9,13},{10,14},{11,15},{16,20},{17,... | collective-permute-start | bytes 786440 | tf_op jit(solution)/shard_map/ppermute | solution.py:20
  107.8 9.8 %collective-permute-start.1 = (bf16[8,64,2,128]{3,1,2,0:T(8,128)(2,1)S(1)}, bf16[8,64,2,128]{3,1,2,0:T(8,128)(2,1)S(1)}, u32[]{:S(2)}, u32[]{:S(2)}) collective-permute-start(bf16[8,64,2,128]{3,1,2,0:T(8,128)(2,1)S(1)} %pad_maximum_fusion), channel_id=1, source_target_pairs={{4,0},{5,1},{6,2},{7,3},{12,8},{13,9},{14,10},{15,11},{20,16},{21,... | collective-permute-start | bytes 786440 | tf_op jit(solution)/shard_map/ppermute | solution.py:21
  118.3 5.9 %collective-permute-start.2 = (bf16[24,16,2,128]{3,1,2,0:T(8,128)(2,1)}, bf16[24,16,2,128]{3,1,2,0:T(8,128)(2,1)S(1)}, u32[]{:S(2)}, u32[]{:S(2)}) collective-permute-start(bf16[24,16,2,128]{3,1,2,0:T(8,128)(2,1)} %get-tuple-element.28), channel_id=1, source_target_pairs={{0,8},{8,16},{16,24},{24,0},{1,9},{9,17},{17,25},{25,1},{2,10},{10... | collective-permute-start | bytes 589832 | tf_op jit(solution)/shard_map/ppermute | solution.py:20
  118.3 6.3 %collective-permute-start.3 = (bf16[24,16,2,128]{3,1,2,0:T(8,128)(2,1)S(1)}, bf16[24,16,2,128]{3,1,2,0:T(8,128)(2,1)S(1)}, u32[]{:S(2)}, u32[]{:S(2)}) collective-permute-start(bf16[24,16,2,128]{3,1,2,0:T(8,128)(2,1)S(1)} %get-tuple-element.27), channel_id=1, source_target_pairs={{8,0},{16,8},{24,16},{0,24},{9,1},{17,9},{25,17},{1,25},{10,2},{18... | collective-permute-start | bytes 589832 | tf_op jit(solution)/shard_map/ppermute | solution.py:21
  130.5 1.0 copy-start.4
  131.3 1.5 copy-start.8
  131.4 1.5 copy-start.9
  131.5 39.6 %copy-start.1 = (f32[8,64,128]{2,1,0:T(8,128)S(1)}, f32[8,64,128]{2,1,0:T(8,128)}, u32[]{:S(2)}) copy-start(f32[8,64,128]{2,1,0:T(8,128)} %reduce-scatter.6.cloned.1.call-done) | copy-start | bytes 786436
  132.7 53.5 %copy-start.11 = (bf16[2,512,512]{2,1,0:T(8,128)(2,1)S(1)}, bf16[2,512,512]{2,1,0:T(8,128)(2,1)}, u32[]{:S(2)}) copy-start(bf16[2,512,512]{2,1,0:T(8,128)(2,1)} %param.16) | copy-start | bytes 3145732
  132.7 53.5 %copy-start.13 = (bf16[2,512,512]{2,1,0:T(8,128)(2,1)S(1)}, bf16[2,512,512]{2,1,0:T(8,128)(2,1)}, u32[]{:S(2)}) copy-start(bf16[2,512,512]{2,1,0:T(8,128)(2,1)} %param.15) | copy-start | bytes 3145732
  132.8 81.6 %reduce-scatter.10.cloned.1.call-start = ((), (), s32[]{:S(2)}) async-start(), calls=%async_computation.7 | async-start | bytes 1310720 | tf_op jit(solution)/shard_map/reduce_scatter | solution.py:119
  188.2 51.9 %copy-start.3 = (bf16[2,512,3,128]{3,1,2,0:T(8,128)(2,1)S(1)}, bf16[2,512,3,128]{3,1,2,0:T(8,128)(2,1)}, u32[]{:S(2)}) copy-start(bf16[2,512,3,128]{3,1,2,0:T(8,128)(2,1)} %param.13) | copy-start | bytes 2359300
  188.2 110.7 %reduce-scatter.12.cloned.1.call-start = ((), (), s32[]{:S(2)}) async-start(), calls=%async_computation.8 | async-start | bytes 1310720 | tf_op jit(solution)/shard_map/reduce_scatter | solution.py:109
  242.6 13.2 %collective-permute-start.4 = (bf16[8,64,2,128]{3,1,2,0:T(8,128)(2,1)S(1)}, bf16[8,64,2,128]{3,1,2,0:T(8,128)(2,1)S(1)}, u32[]{:S(2)}, u32[]{:S(2)}) collective-permute-start(bf16[8,64,2,128]{3,1,2,0:T(8,128)(2,1)S(1)} %pad_maximum_fusion.1), channel_id=1, source_target_pairs={{0,4},{1,5},{2,6},{3,7},{8,12},{9,13},{10,14},{11,15},{16,20},{17,... | collective-permute-start | bytes 786440 | tf_op jit(solution)/shard_map/ppermute | solution.py:20
  246.1 9.7 %collective-permute-start.5 = (bf16[8,64,2,128]{3,1,2,0:T(8,128)(2,1)S(1)}, bf16[8,64,2,128]{3,1,2,0:T(8,128)(2,1)S(1)}, u32[]{:S(2)}, u32[]{:S(2)}) collective-permute-start(bf16[8,64,2,128]{3,1,2,0:T(8,128)(2,1)S(1)} %pad_maximum_fusion.1), channel_id=1, source_target_pairs={{4,0},{5,1},{6,2},{7,3},{12,8},{13,9},{14,10},{15,11},{20,16},{21,... | collective-permute-start | bytes 786440 | tf_op jit(solution)/shard_map/ppermute | solution.py:21
  256.6 5.6 %collective-permute-start.6 = (bf16[24,16,2,128]{3,1,2,0:T(8,128)(2,1)}, bf16[24,16,2,128]{3,1,2,0:T(8,128)(2,1)S(1)}, u32[]{:S(2)}, u32[]{:S(2)}) collective-permute-start(bf16[24,16,2,128]{3,1,2,0:T(8,128)(2,1)} %get-tuple-element.24), channel_id=1, source_target_pairs={{0,8},{8,16},{16,24},{24,0},{1,9},{9,17},{17,25},{25,1},{2,10},{10... | collective-permute-start | bytes 589832 | tf_op jit(solution)/shard_map/ppermute | solution.py:20
  256.6 6.5 %collective-permute-start.7 = (bf16[24,16,2,128]{3,1,2,0:T(8,128)(2,1)}, bf16[24,16,2,128]{3,1,2,0:T(8,128)(2,1)S(1)}, u32[]{:S(2)}, u32[]{:S(2)}) collective-permute-start(bf16[24,16,2,128]{3,1,2,0:T(8,128)(2,1)} %get-tuple-element.23), channel_id=1, source_target_pairs={{8,0},{16,8},{24,16},{0,24},{9,1},{17,9},{25,17},{1,25},{10,2},{18... | collective-permute-start | bytes 589832 | tf_op jit(solution)/shard_map/ppermute | solution.py:21
  269.0 1.0 copy-start.5
  271.2 53.5 %copy-start.12 = (bf16[2,512,512]{2,1,0:T(8,128)(2,1)S(1)}, bf16[2,512,512]{2,1,0:T(8,128)(2,1)}, u32[]{:S(2)}) copy-start(bf16[2,512,512]{2,1,0:T(8,128)(2,1)} %param.16) | copy-start | bytes 3145732
  271.2 53.5 %copy-start.14 = (bf16[2,512,512]{2,1,0:T(8,128)(2,1)S(1)}, bf16[2,512,512]{2,1,0:T(8,128)(2,1)}, u32[]{:S(2)}) copy-start(bf16[2,512,512]{2,1,0:T(8,128)(2,1)} %param.15) | copy-start | bytes 3145732
  271.2 81.5 %reduce-scatter.14.cloned.1.call-start = ((), (), s32[]{:S(2)}) async-start(), calls=%async_computation.9 | async-start | bytes 1310720 | tf_op jit(solution)/shard_map/reduce_scatter | solution.py:119
  326.6 74.4 %copy-start.6 = (bf16[1,512,128]{2,1,0:T(8,128)(2,1)S(1)}, bf16[1,512,128]{2,1,0:T(8,128)(2,1)}, u32[]{:S(2)}) copy-start(bf16[1,512,128]{2,1,0:T(8,128)(2,1)} %param.20) | copy-start | bytes 393220
  326.6 74.4 %all-gather.2.cloned.1.call-start = ((), (), s32[]{:S(2)}) async-start(), calls=%async_computation.10 | async-start | bytes 2621440 | tf_op jit(solution)/shard_map/all_gather | solution.py:170
Sparse Core Ops, SparseCore 0:
  11.2 75.0 reduce-scatter.5
  132.9 27.4 reduce-scatter.7
  188.3 26.0 reduce-scatter.9
  271.3 27.5 reduce-scatter.11
  326.7 26.0 reduce-scatter.13
  379.3 21.6 all-gather.1
where the time goes:
time: 412 us; the launch traced here: 411 us
  waiting for transfers between devices  210 us (51%)
  blocking collectives  109 us (26%)
  between operations  28.2 us (7%)
  local copies, waits for them, and re-layouts  18.4 us (4%)
  other arithmetic  17.5 us (4%)
  matrix products  14.6 us (4%)
  starting transfers between devices  13 us (3%)
    reduce_scatter x1, waiting for transfers between devices, per_device(): lax.psum_scatter(partial_value, ('sect', 'var'), scatter_dimension=1, til...  73.2 us
    reduce_scatter x2, waiting for transfers between devices, layer_heads(): lax.psum_scatter(partial_value, 'var', scatter_dimension=2, tiled=True)  55.1 us
    reduce_scatter x2, waiting for transfers between devices, layer_heads(): fed = lax.psum_scatter(part_fed, 'var', scatter_dimension=2, tiled=True)  52.3 us
    all_gather x2, blocking collectives, layer_heads(): gathered = lax.all_gather(stream, 'var', axis=2, tiled=True)  28.6 us
    all_gather x2, blocking collectives, layer_heads(): widened = lax.all_gather(attn_stream, 'var', axis=2, tiled=True)  27.9 us
    all_gather x1, waiting for transfers between devices, per_device(): lax.all_gather(gathered, 'sect', axis=1, tiled=True)  21.8 us
    psum x2, blocking collectives, layer_heads(): lax.psum((jnp.sum(mixed_sum, axis=-1), jnp.sum(mixed_sum * mixed_sum, axi...  19.1 us
    psum x2, blocking collectives, layer_heads(): lax.psum((jnp.sum(fed, axis=-1), jnp.sum(fed * fed, axis=-1)), 'var')  19.1 us
  transfers between devices with their start and end apart: 14, of which 10 were waited for; matrix products, arithmetic and copies ran while one was open for 2% of the time, Pallas kernels for 0%

commit v1 on v0

v1 whole, which is shorter than its diff:
```python
import functools
import jax
import jax.numpy as jnp
from jax import lax
from jax.experimental import pallas as pl
from jax.experimental.pallas import tpu as pltpu
from jax.sharding import PartitionSpec as P

WL = 8
WW = 16
HD = 64
MESH = pl.DeviceIdType.MESH

epsilon = 1e-06


def extended(array, sides, width, wrap):
    for axis, dim in sides:
        size, length = (lax.axis_size(axis), array.shape[dim])
        up = [(i, (i + 1) % size) for i in range(size if wrap else size - 1)]
        down = [(j, i) for i, j in up]
        last = lax.slice_in_dim(array, length - width, length, axis=dim)
        initial = lax.slice_in_dim(array, 0, width, axis=dim)
        before = lax.ppermute(last, axis, up)
        after = lax.ppermute(initial, axis, down)
        array = jnp.concatenate([before, array, after], axis=dim)
    return array


def to_windows(frame, win_rows, win_cols, heads_local, head_dim):
    shaped = frame.reshape(win_rows, WL, win_cols, WW, heads_local, head_dim)
    return shaped.transpose(0, 2, 1, 3, 4, 5).reshape(
        win_rows, win_cols, WL * WW, heads_local, head_dim
    )


def attend(queries, paired, head_scale, shift_lat, shift_lon, heads_local, head_dim):
    lat_rows, lon_cols, head_cols = queries.shape
    query_pad = jnp.pad(queries, ((WL, WL), (WW, WW), (0, 0)))
    frame_rows = lat_rows + WL
    frame_cols = lon_cols + WW
    win_rows = frame_rows // WL
    win_cols = frame_cols // WW
    q_frame = lax.dynamic_slice(
        query_pad, (shift_lat, shift_lon, 0), (frame_rows, frame_cols, head_cols)
    )
    kv_frame = lax.dynamic_slice(
        paired, (shift_lat, shift_lon, 0), (frame_rows, frame_cols, 2 * head_cols)
    )
    q_win = to_windows(q_frame, win_rows, win_cols, heads_local, head_dim)
    k_win = to_windows(kv_frame[:, :, :head_cols], win_rows, win_cols, heads_local, head_dim)
    v_win = to_windows(kv_frame[:, :, head_cols:], win_rows, win_cols, heads_local, head_dim)
    scores = (
        jnp.einsum("wnqhe,wnkhe->wnhqk", q_win, k_win, preferred_element_type=jnp.float32)
        * head_scale[:, None, None]
    )
    lat_total = lat_rows * lax.axis_size("lat")
    global_row = (
        lax.axis_index("lat") * lat_rows - WL + shift_lat + jnp.arange(frame_rows, dtype=jnp.int32)
    )
    usable = (global_row >= 0) & (global_row < lat_total)
    usable = jnp.broadcast_to(
        usable.reshape(win_rows, 1, WL, 1), (win_rows, win_cols, WL, WW)
    ).reshape(win_rows, win_cols, 1, 1, WL * WW)
    scores = jnp.where(usable, scores, -1e30)
    top = jnp.max(scores, axis=-1, keepdims=True)
    expo = jnp.exp(scores - top)
    weights = (expo / jnp.sum(expo, axis=-1, keepdims=True)).astype(jnp.bfloat16)
    attended = jnp.einsum(
        "wnhqk,wnkhe->wnqhe", weights, v_win, preferred_element_type=jnp.float32
    ).astype(jnp.bfloat16)
    attended = (
        attended.reshape(win_rows, win_cols, WL, WW, head_cols)
        .transpose(0, 2, 1, 3, 4)
        .reshape(frame_rows, frame_cols, head_cols)
    )
    return lax.dynamic_slice(
        attended, (WL - shift_lat, WW - shift_lon, 0), (lat_rows, lon_cols, head_cols)
    )


def dot(a, b):
    return jnp.dot(a, b, preferred_element_type=jnp.float32)


def greet(axes):
    barrier = pltpu.get_barrier_semaphore()
    total = 0
    for axis in axes:
        size = lax.axis_size(axis)
        me = lax.axis_index(axis)
        for d in range(1, size):
            pl.semaphore_signal(
                barrier, inc=1, device_id={axis: lax.rem(me + d, size)}, device_id_type=MESH
            )
            total += 1
    pl.semaphore_wait(barrier, total)


def send(src, dst, sems, phase, d, axis, target):
    send_sem, recv_sem = sems
    copy = pltpu.make_async_remote_copy(
        src_ref=src,
        dst_ref=dst,
        send_sem=send_sem.at[phase, d],
        recv_sem=recv_sem.at[phase, d],
        device_id={axis: target},
        device_id_type=MESH,
    )
    copy.start()
    return copy


def ring(axis):
    size = lax.axis_size(axis)
    me = lax.axis_index(axis)
    after = [lax.rem(me + d, size) for d in range(size)]
    before = [lax.rem(me + size - d, size) for d in range(size)]
    return size, me, after, before


def head_unit(x):
    lane = lax.broadcasted_iota(jnp.int32, x.shape, 1)
    square = x * x
    inverse = jnp.zeros_like(x)
    for head in range(x.shape[1] // HD):
        mine = (lane >= head * HD) & (lane < (head + 1) * HD)
        total = jnp.sum(jnp.where(mine, square, 0.0), axis=1, keepdims=True)
        inverse = jnp.where(mine, lax.rsqrt(total + epsilon), inverse)
    return x * inverse


def project_chunk(x, wqkv_ref, q_ref, kv_ref, owner):
    rows, cols = x.shape[0], q_ref.shape[1]
    projected = dot(x, wqkv_ref[...])
    at = pl.ds(pl.multiple_of(owner * rows, rows), rows)
    q_ref[at, :] = head_unit(projected[:, :cols]).astype(jnp.bfloat16)
    kv_ref[at, :cols] = head_unit(projected[:, cols : 2 * cols]).astype(jnp.bfloat16)
    kv_ref[at, cols:] = projected[:, 2 * cols :].astype(jnp.bfloat16)


def norm_add(stream, x, gain, bias):
    width = x.shape[1]
    mean = jnp.sum(x, axis=1, keepdims=True) / width
    variance = jnp.sum(x * x, axis=1, keepdims=True) / width - mean * mean
    normed = (x - mean) * lax.rsqrt(variance + 1e-05)
    return (stream.astype(jnp.float32) + gain * normed + bias).astype(jnp.bfloat16)


def embed_kernel(
    patches, table, params, wqkv, q_ref, kv_ref, x_ref, params_ref,
    patch_in, table_in, params_in, part, part_in, full, send_sem, recv_sem,
):
    sems = (send_sem, recv_sem)
    sects, my_sect, to_sect, _ = ring("sect")
    vars_, my_var, to_var, from_var = ring("var")
    lat_rows, lon_total, depth = patches.shape
    cols = lon_total // sects
    rows = full.shape[1]
    greet(("sect", "var"))
    copies = []
    moved = []
    for d in range(1, sects):
        t = to_sect[d]
        moved.append(send(table, table_in.at[d - 1], sems, 0, d, "sect", t))
        moved.append(
            send(
                patches.at[:, pl.ds(pl.multiple_of(t * cols, cols), cols), :],
                patch_in.at[d - 1], sems, 1, d, "sect", t,
            )
        )
    params_in[my_var] = params[...]
    for d in range(1, vars_):
        copies.append(
            send(params, params_in.at[my_var], sems, 2, d, "var", to_var[d])
        )
    for copy in moved:
        copy.wait()
    weights = jnp.concatenate([table[...]] + [table_in[d] for d in range(sects - 1)], axis=0)
    per = rows // cols

    def partial_of(owner):
        lat = pl.ds(owner * per, per)
        own = patches[lat, pl.ds(pl.multiple_of(my_sect * cols, cols), cols), :]
        blocks = [own] + [patch_in[d, lat] for d in range(sects - 1)]
        x = jnp.concatenate([b.reshape(rows, depth) for b in blocks], axis=1)
        return dot(x, weights)

    outgoing = []
    for d in range(1, vars_):
        part[d - 1] = partial_of(to_var[d]).astype(jnp.bfloat16)
        outgoing.append(send(part.at[d - 1], part_in.at[d - 1], sems, 3, d, "var", to_var[d]))
    total = partial_of(my_var)
    for d in range(1, vars_):
        outgoing[d - 1].wait()
        total = total + part_in[d - 1].astype(jnp.float32)
    full[my_var] = total.astype(jnp.bfloat16)
    gather_project(full, wqkv, q_ref, kv_ref, sems, 4)
    x_ref[...] = full[...]
    for copy in copies:
        copy.wait()
    params_ref[...] = params_in[...]


def gather_project(full, wqkv, q_ref, kv_ref, sems, phase):
    vars_, my_var, to_var, from_var = ring("var")
    outgoing = [
        send(full.at[my_var], full.at[my_var], sems, phase, d, "var", to_var[d])
        for d in range(1, vars_)
    ]
    project_chunk(full[my_var], wqkv, q_ref, kv_ref, my_var)
    for d in range(1, vars_):
        outgoing[d - 1].wait()
        project_chunk(full[from_var[d]], wqkv, q_ref, kv_ref, from_var[d])


def layer_body(
    layer, attended, wout, x_ref, params, w_in, w_out, part, part_in, mid, back, back_in, full, sems
):
    vars_, my_var, to_var, from_var = ring("var")
    rows = mid.shape[1]

    def chosen(kind, position):
        index = (kind * 2 + layer) * 2 + position
        return jnp.concatenate([params[v, index : index + 1, :] for v in range(vars_)], axis=1)

    def mixed_of(owner):
        at = pl.ds(pl.multiple_of(owner * rows, rows), rows)
        return dot(attended[at, :], wout[...])

    def fed_of(x):
        hidden = jax.nn.gelu(dot(x, w_in[...]), approximate=True).astype(jnp.bfloat16)
        return dot(hidden, w_out[...])

    outgoing = []
    for d in range(1, vars_):
        part[d - 1] = mixed_of(to_var[d]).astype(jnp.bfloat16)
        outgoing.append(send(part.at[d - 1], part_in.at[d - 1], sems, 0, d, "var", to_var[d]))
    total = mixed_of(my_var)
    for d in range(1, vars_):
        outgoing[d - 1].wait()
        total = total + part_in[d - 1].astype(jnp.float32)
    mid[my_var] = norm_add(x_ref[my_var], total, chosen(0, 0), chosen(1, 0))
    outgoing = [
        send(mid.at[my_var], mid.at[my_var], sems, 1, d, "var", to_var[d])
        for d in range(1, vars_)
    ]
    total = fed_of(mid[my_var])
    returned = []
    for d in range(1, vars_):
        outgoing[d - 1].wait()
        back[d - 1] = fed_of(mid[from_var[d]]).astype(jnp.bfloat16)
        returned.append(send(back.at[d - 1], back_in.at[d - 1], sems, 2, d, "var", from_var[d]))
    for d in range(1, vars_):
        returned[d - 1].wait()
        total = total + back_in[d - 1].astype(jnp.float32)
    full[my_var] = norm_add(mid[my_var], total, chosen(0, 1), chosen(1, 1))


def layer_kernel(
    layer, attended, wout, x_ref, params, w_in, w_out, wqkv, q_ref, kv_ref, out_ref,
    part, part_in, mid, back, back_in, full, send_sem, recv_sem,
):
    sems = (send_sem, recv_sem)
    greet(("var",))
    layer_body(
        layer, attended, wout, x_ref, params, w_in, w_out, part, part_in, mid, back, back_in, full, sems
    )
    gather_project(full, wqkv, q_ref, kv_ref, sems, 3)
    out_ref[...] = full[...]


def last_kernel(
    layer, attended, wout, x_ref, params, w_in, w_out, table, out_ref,
    part, part_in, mid, back, back_in, full, table_in, made, landed, send_sem, recv_sem,
):
    sems = (send_sem, recv_sem)
    sects, my_sect, to_sect, from_sect = ring("sect")
    vars_, my_var, to_var, from_var = ring("var")
    rows = full.shape[1]
    lat_rows, lon_total, depth = out_ref.shape
    cols = lon_total // sects
    per = rows // cols
    greet(("sect", "var"))
    tables = [
        send(table, table_in.at[d - 1], sems, 4, d, "sect", to_sect[d]) for d in range(1, sects)
    ]
    layer_body(
        layer, attended, wout, x_ref, params, w_in, w_out, part, part_in, mid, back, back_in, full, sems
    )
    outgoing = [
        send(full.at[my_var], full.at[my_var], sems, 3, d, "var", to_var[d])
        for d in range(1, vars_)
    ]
    for copy in tables:
        copy.wait()
    weights = jnp.concatenate([table[...]] + [table_in[d] for d in range(sects - 1)], axis=1)
    for k in range(vars_):
        if k:
            outgoing[k - 1].wait()
        owner = from_var[k]
        decoded = dot(full[owner], weights).astype(jnp.bfloat16)
        for d in range(sects):
            made[d, pl.ds(owner * per, per)] = decoded[:, d * depth : (d + 1) * depth].reshape(
                per, cols, depth
            )
    copies = []
    for d in range(1, sects):
        copies.append(
            send(made.at[d], landed.at[sects - d], sems, 5, d, "sect", from_sect[d])
        )
    out_ref[:, pl.ds(pl.multiple_of(my_sect * cols, cols), cols), :] = made[0]
    for d in range(1, sects):
        copies[d - 1].wait()
        block = to_sect[d]
        out_ref[:, pl.ds(pl.multiple_of(block * cols, cols), cols), :] = landed[sects - d]


def per_device(
    patches,
    embed_weight,
    qkv_weight,
    out_weight,
    mlp_in_weight,
    mlp_out_weight,
    logit_scale,
    norm_gain,
    norm_bias,
    decode_weight,
    shifts,
):
    _, lat_rows, lon_total, patch_dim = patches.shape
    width = embed_weight.shape[2]
    layers, _, _, head_cols = qkv_weight.shape
    sects, vars_ = lax.axis_size("sect"), lax.axis_size("var")
    cols = lon_total // sects
    tokens = lat_rows * cols
    rows = tokens // vars_
    hidden = mlp_in_weight.shape[2]
    bf = jnp.bfloat16
    vmem = pl.BlockSpec(memory_space=pltpu.VMEM)
    wqkv = [qkv_weight[layer].reshape(width, 3 * head_cols) for layer in range(layers)]
    params = jnp.concatenate(
        [norm_gain.reshape(2 * layers, -1), norm_bias.reshape(2 * layers, -1)], axis=0
    )

    def call(kernel, cid, outs, scratch, phases, *args):
        return pl.pallas_call(
            kernel,
            out_shape=outs,
            in_specs=[vmem] * len(args),
            out_specs=jax.tree.map(lambda _: vmem, outs),
            scratch_shapes=scratch
            + [pltpu.SemaphoreType.DMA((phases, 4)), pltpu.SemaphoreType.DMA((phases, 4))],
            compiler_params=pltpu.CompilerParams(
                collective_id=cid, has_side_effects=True, vmem_limit_bytes=40 * 1024 * 1024
            ),
        )(*args)

    qkv_outs = [
        jax.ShapeDtypeStruct((tokens, head_cols), bf),
        jax.ShapeDtypeStruct((tokens, 2 * head_cols), bf),
        jax.ShapeDtypeStruct((vars_, rows, width), bf),
    ]
    q, kv, x, params = call(
        embed_kernel, 0,
        qkv_outs + [jax.ShapeDtypeStruct((vars_,) + params.shape, jnp.float32)],
        [
            pltpu.VMEM((sects - 1, lat_rows, cols, patch_dim), bf),
            pltpu.VMEM((sects - 1, patch_dim, width), bf),
            pltpu.VMEM((vars_,) + params.shape, jnp.float32),
            pltpu.VMEM((vars_ - 1, rows, width), bf),
            pltpu.VMEM((vars_ - 1, rows, width), bf),
            pltpu.VMEM((vars_, rows, width), bf),
        ],
        5, patches[0], embed_weight[0], params, wqkv[0],
    )
    slots = [
        pltpu.VMEM((vars_ - 1, rows, width), bf),
        pltpu.VMEM((vars_ - 1, rows, width), bf),
        pltpu.VMEM((vars_, rows, width), bf),
        pltpu.VMEM((vars_ - 1, rows, width), bf),
        pltpu.VMEM((vars_ - 1, rows, width), bf),
        pltpu.VMEM((vars_, rows, width), bf),
    ]
    for layer in range(layers):
        paired = kv.reshape(lat_rows, cols, 2 * head_cols)
        paired = extended(paired, (("lat", 0),), WL, False)
        paired = extended(paired, (("sect", 1),), WW, True)
        attended = attend(
            q.reshape(lat_rows, cols, head_cols), paired, logit_scale[layer],
            shifts[layer, 0], shifts[layer, 1], head_cols // HD, HD,
        ).reshape(tokens, head_cols)
        args = (
            attended, out_weight[layer], x, params, mlp_in_weight[layer], mlp_out_weight[layer]
        )
        if layer + 1 < layers:
            q, kv, x = call(
                functools.partial(layer_kernel, layer), 1 + layer, qkv_outs, slots, 4,
                *args, wqkv[layer + 1],
            )
    out = call(
        functools.partial(last_kernel, layers - 1), layers,
        jax.ShapeDtypeStruct((lat_rows, lon_total, patch_dim), bf),
        slots
        + [
            pltpu.VMEM((sects - 1, width, patch_dim), bf),
            pltpu.VMEM((sects, lat_rows, cols, patch_dim), bf),
            pltpu.VMEM((sects, lat_rows, cols, patch_dim), bf),
        ],
        6, *args, decode_weight[0],
    )
    return out[None]


def solution(mesh):
    return jax.shard_map(
        per_device,
        mesh=mesh,
        in_specs=(
            P(("sect", "var"), "lat", None, None),
            P(("sect", "var"), None, None),
            P(None, None, None, "var"),
            P(None, "var", None),
            P(None, None, "var"),
            P(None, "var", None),
            P(None, "var"),
            P(None, None, "var"),
            P(None, None, "var"),
            P(("sect", "var"), None, None),
            P(),
        ),
        out_specs=P(("sect", "var"), "lat", None, None),
        check_vma=False,
    )
```

time: 412 us -> 257 us (0.62)
  waiting for transfers between devices: 210 us -> 8.99 us
  Pallas kernels: 0 us -> 163 us
  blocking collectives: 109 us -> 0 us
  local copies, waits for them, and re-layouts: 18.4 us -> 35 us
  between operations: 28.2 us -> 14.1 us
  other arithmetic: 17.5 us -> 7.15 us
    reduce_scatter x5 -> x0, waiting for transfers between devices: 181 us -> none  [the longest x1 73.2 us: per_device(): lax.psum_scatter(partial_value, ('sect', 'var'), scatter_dimension=1, til...]
    pallas_call x0 -> x3, Pallas kernels: none -> 163 us  [call(): pl.pallas_call(kernel, out_shape=outs, in_specs=[vmem] * len(args), out_s...]
    all_gather x5 -> x0, blocking collectives: 70.9 us -> none  [the longest x2 28.6 us: layer_heads(): gathered = lax.all_gather(stream, 'var', axis=2, tiled=True)]
    psum x4 -> x0, blocking collectives: 38.2 us -> none  [the longest x2 19.1 us: layer_heads(): lax.psum((jnp.sum(mixed_sum, axis=-1), jnp.sum(mixed_sum * mixed_sum, axi...]
    all_gather x1 -> x0, waiting for transfers between devices: 21.8 us -> none  [per_device(): lax.all_gather(gathered, 'sect', axis=1, tiled=True)]
    dot_general x8 -> x0, matrix products: 11 us -> none  [the longest x2 3.78 us: layer_heads(): jnp.einsum('rlf,fd->rld', hidden, w_out, preferred_element_type=jnp.float32)]
    reduce_sum x8 -> x0, other arithmetic: 7.07 us -> none  [the longest x4 2.45 us: unit_norm(): jnp.sum(shaped * shaped, axis=-1, keepdims=True) + epsilon]
    reshape x2 -> x6, local copies, waits for them, and re-layouts: 0.59 us -> 7.25 us  [to_windows(): shaped = frame.reshape(win_rows, WL, win_cols, WW, heads_local, head_dim)]
  transfers between devices with their start and end apart: 14 -> 8, of which waited for: 10 -> 4; matrix products, arithmetic and copies ran while one was open for 2% -> 6% of each run, Pallas kernels for 0% -> 0%
where the time goes in v1:
time: 257 us; the launch traced here: 255 us
  Pallas kernels  163 us (63%)
  local copies, waits for them, and re-layouts  35 us (14%)
  starting transfers between devices  14.3 us (6%)
  between operations  14.1 us (5%)
  matrix products  12.6 us (5%)
  waiting for transfers between devices  8.99 us (3%)
  other arithmetic  7.15 us (3%)
    pallas_call x3, Pallas kernels, call(): pl.pallas_call(kernel, out_shape=outs, in_specs=[vmem] * len(args), out_s...  163 us
    ppermute x4, starting transfers between devices, extended(): before = lax.ppermute(last, axis, up)  11.5 us
    reshape x6, local copies, waits for them, and re-layouts, to_windows(): shaped = frame.reshape(win_rows, WL, win_cols, WW, heads_local, head_dim)  7.25 us
    transpose x6, local copies, waits for them, and re-layouts, to_windows(): shaped.transpose(0, 2, 1, 3, 4, 5)  6.59 us
    concatenate x4, other arithmetic, extended(): array = jnp.concatenate([before, array, after], axis=dim)  6.55 us
    dot_general x2, matrix products, attend(): jnp.einsum('wnhqk,wnkhe->wnqhe', weights, v_win, preferred_element_type=j...  5.4 us
    ppermute x4, waiting for transfers between devices, extended(): after = lax.ppermute(initial, axis, down)  5.28 us
  transfers between devices with their start and end apart: 8, of which 4 were waited for; matrix products, arithmetic and copies ran while one was open for 6% of the time, Pallas kernels for 0%

profile of v1, /device:TPU:0, one launch (start us, length us, event | category | flops | bytes accessed | tf_op | source)
XLA Modules:
  0.0 255.4 jit_solution(6764309082710864782)
XLA Ops:
  0.0 1.2 fusion.20
  1.3 0.2 copy.68
  1.4 0.2 copy.39.wqkv
  1.7 40.8 %shard_map.109 = (bf16[512,128]{1,0:T(8,128)(2,1)S(1)}, bf16[512,256]{1,0:T(8,128)(2,1)S(1)}, bf16[4,128,512]{2,1,0:T(8,128)(2,1)S(1)}, f32[4,8,128]{2,1,0:T(8,128)S(1)}) custom-call(bf16[8,256,128]{2,1,0:T(8,128)(2,1)S(1)} %bitcast.77, bf16[128,512]{1,0:T(8,128)(2,1)S(1)} %bitcast.81, f32[8,128]{1,0:T(8,128)S(1)} %pad_maximum_fusion.6.params, ...), custom_call_target="tpu_custom_call" | custom-call | tf_op jit(solution)/shard_map/pallas_call | solution.py:348
  42.5 1.3 collective-permute-start.1
  43.8 5.9 %collective-permute-start = (bf16[8,64,256]{2,1,0:T(8,128)(2,1)S(1)}, bf16[8,64,256]{2,1,0:T(8,128)(2,1)}, u32[]{:S(2)}, u32[]{:S(2)}) collective-permute-start(bf16[8,64,256]{2,1,0:T(8,128)(2,1)S(1)} %bitcast.68), channel_id=1, source_target_pairs={{0,4},{1,5},{2,6},{3,7},{8,12},{9,13},{10,14},{11,15},{16,20},{17,... | collective-permute-start | bytes 786440 | tf_op jit(solution)/shard_map/ppermute | solution.py:24
  49.8 0.6 fusion.23
  55.5 1.7 slice_bitcast_fusion
  57.2 1.1 pad_dynamic-slice_fusion.11
  58.3 0.6 compare_and_fusion
  61.4 0.1 broadcast_in_dim.39
  61.5 0.7 broadcast_in_dim.40
  62.2 0.9 copy.69
  63.1 1.2 copy.50.wqkv
  64.3 2.1 reshape.108
  66.4 2.1 copy.41
  68.5 1.0 slice_bitcast_fusion.4
  69.5 1.0 pad_maximum_fusion.3
  70.5 0.1 collective-permute-start.3
  70.5 0.5 collective-permute-start.2
  71.0 1.3 slice_bitcast_fusion.6
  72.3 2.9 %collective-permute-done.3 = bf16[24,16,256]{2,1,0:T(8,128)(2,1)S(1)} collective-permute-done((bf16[24,16,256]{2,1,0:T(8,128)(2,1)S(1)}, bf16[24,16,256]{2,1,0:T(8,128)(2,1)S(1)}, u32[]{:S(2)}, u32[]{:S(2)}) %collective-permute-start.3) | collective-permute-done | bytes 196640 | tf_op jit(solution)/shard_map/ppermute | solution.py:25
  75.2 2.2 collective-permute-done.2
  77.5 2.2 fusion.15
  79.6 1.0 fusion.22
  80.6 2.1 reshape.110
  82.7 2.1 copy.42
  84.8 1.9 fusion.24
  86.8 2.9 %fusion.7 = f32[2,5,2,128,128]{3,4,2,1,0:T(8,128)} fusion(bf16[2,5,128,2,64]{4,2,3,1,0:T(8,128)(2,1)} %bitcast.89, bf16[2,5,128,2,64]{4,2,3,1,0:T(8,128)(2,1)} %bitcast.95, f32[2]{0:T(128)S(1)} %copy-done.10, pred[2,128]{1,0:T(4,128)(4,1)S(1)} %copy-done.8), kind=kOutput, calls=%fused_computation.9 | convolution fusion | flops 42598400 | bytes 1966344 | tf_op jit(solution)/shard_map/wnqhe,wnkhe->wnhqk/dot_general | solution.py:54
  89.7 2.1 reshape.105
  91.8 2.1 copy.40
  93.9 3.2 %fusion.8 = bf16[2,5,128,2,64]{2,4,3,1,0:T(8,128)(2,1)} fusion(bf16[2,5,128,2,64]{4,2,3,1,0:T(8,128)(2,1)} %bitcast.100, f32[2,5,2,128]{3,2,1,0:T(2,128)S(1)} %fusion.24, f32[2,5,2,128,128]{3,4,2,1,0:T(8,128)} %fusion.7), kind=kOutput, calls=%fused_computation.14 | convolution fusion | flops 43092608 | bytes 1976320 | tf_op jit(solution)/shard_map/wnhqk,wnkhe->wnqhe/dot_general | solution.py:69
  97.0 2.1 copy.47
  99.1 2.1 reshape.112
  101.3 1.0 copy.48
  102.3 57.8 %shard_map.110 = (bf16[512,128]{1,0:T(8,128)(2,1)S(1)}, bf16[512,256]{1,0:T(8,128)(2,1)S(1)}, bf16[4,128,512]{2,1,0:T(8,128)(2,1)S(1)}) custom-call(bf16[512,128]{1,0:T(8,128)(2,1)S(1)} %bitcast.75, bf16[128,512]{1,0:T(8,128)(2,1)S(1)} %get-tuple-element.34.wout, bf16[4,128,512]{2,1,0:T(8,128)(2,1)S(1)} %get-tuple-element.14.x_ref, ...), custom_call_target="tpu_custom_call" | custom-call | tf_op jit(solution)/shard_map/pallas_call | solution.py:348
  160.1 0.8 copy-done
  160.9 0.6 copy-done.4
  161.5 1.4 collective-permute-start.5
  163.0 4.6 %collective-permute-start.4 = (bf16[8,64,256]{2,1,0:T(8,128)(2,1)S(1)}, bf16[8,64,256]{2,1,0:T(8,128)(2,1)S(1)}, u32[]{:S(2)}, u32[]{:S(2)}) collective-permute-start(bf16[8,64,256]{2,1,0:T(8,128)(2,1)S(1)} %bitcast.72), channel_id=1, source_target_pairs={{0,4},{1,5},{2,6},{3,7},{8,12},{9,13},{10,14},{11,15},{16,20},{17,... | collective-permute-start | bytes 786440 | tf_op jit(solution)/shard_map/ppermute | solution.py:24
  167.5 2.4 collective-permute-done.5
  169.9 1.5 collective-permute-done.4
  171.4 0.8 pad_maximum_fusion
  172.2 0.5 collective-permute-start.6
  177.6 0.7 broadcast_in_dim.43
  178.3 0.1 broadcast_in_dim.44
  179.7 0.4 pad_dynamic-slice_fusion.10
  180.1 0.3 reshape.119
  180.4 0.1 copy.52
  180.5 2.6 %fusion.11 = bf16[16,80,256]{2,1,0:T(8,128)(2,1)S(1)} fusion(s32[]{:T(128)S(6)} %select_n.40, s32[]{:T(128)S(6)} %select_n.41, bf16[24,16,256]{2,1,0:T(8,128)(2,1)} %collective-permute-done.6, bf16[8,64,256]{2,1,0:T(8,128)(2,1)S(1)} %collective-permute-done.4, bf16[8,64,256]{2,1,0:T(8,128)(2,1)S(1)} %bitcast.74, ...), kind=kLoop, calls=%fused_computation.27 | loop fusion | flops 3276800 | bytes 1835016 | tf_op jit(solution)/shard_map/concatenate | solution.py:26
  183.1 0.1 fusion.21
  183.3 0.3 reshape.121
  183.6 0.1 copy.53
  183.7 0.2 copy-done.9
  183.9 0.7 fusion.25
  184.5 1.7 fusion.6
  186.2 0.3 reshape.116
  186.5 0.1 copy.51
  186.6 2.2 fusion.9
  188.9 0.5 copy.58
  189.4 0.3 reshape.123
  189.8 0.1 copy-done.1
  189.9 64.7 %shard_map.111 = bf16[8,256,128]{2,1,0:T(8,128)(2,1)S(1)} custom-call(bf16[512,128]{1,0:T(8,128)(2,1)S(1)} %bitcast.76, bf16[128,512]{1,0:T(8,128)(2,1)S(1)} %get-tuple-element.33.wout, bf16[4,128,512]{2,1,0:T(8,128)(2,1)S(1)} %copy-done.1, f32[4,8,128]{2,1,0:T(8,128)S(1)} %get-tuple-element.15.params, bf16[512,512]{1,0:T(8,128)(2,1)S(1)} %get-tuple-element.44.w_in, ...), custom_call_target="tpu_custom_call" | custom-call | tf_op jit(solution)/shard_map/pallas_call | solution.py:348
  254.6 0.8 copy.71
  (31 shorter events, 0.2 us)
Async XLA Ops:
  0.0 1.7 copy-start.11
  0.0 1.7 copy-start.12
  0.0 1.7 copy-start.6
  0.0 1.7 copy-start.2
  1.2 48.5 %copy-start.7 = (s32[2,2]{1,0:T(2,128)S(1)}, s32[2,2]{1,0:T(2,128)}, u32[]{:S(2)}) copy-start(s32[2,2]{1,0:T(2,128)} %param.21) | copy-start | bytes 52
  42.5 26.9 %collective-permute-start.1 = (bf16[8,64,256]{2,1,0:T(8,128)(2,1)S(1)}, bf16[8,64,256]{2,1,0:T(8,128)(2,1)}, u32[]{:S(2)}, u32[]{:S(2)}) collective-permute-start(bf16[8,64,256]{2,1,0:T(8,128)(2,1)S(1)} %bitcast.67), channel_id=1, source_target_pairs={{4,0},{5,1},{6,2},{7,3},{12,8},{13,9},{14,10},{15,11},{20,16},{21,... | collective-permute-start | bytes 786440 | tf_op jit(solution)/shard_map/ppermute | solution.py:25
  43.8 25.7 %collective-permute-start = (bf16[8,64,256]{2,1,0:T(8,128)(2,1)S(1)}, bf16[8,64,256]{2,1,0:T(8,128)(2,1)}, u32[]{:S(2)}, u32[]{:S(2)}) collective-permute-start(bf16[8,64,256]{2,1,0:T(8,128)(2,1)S(1)} %bitcast.68), channel_id=1, source_target_pairs={{0,4},{1,5},{2,6},{3,7},{8,12},{9,13},{10,14},{11,15},{16,20},{17,... | collective-permute-start | bytes 786440 | tf_op jit(solution)/shard_map/ppermute | solution.py:24
  70.5 4.7 %collective-permute-start.3 = (bf16[24,16,256]{2,1,0:T(8,128)(2,1)S(1)}, bf16[24,16,256]{2,1,0:T(8,128)(2,1)S(1)}, u32[]{:S(2)}, u32[]{:S(2)}) collective-permute-start(bf16[24,16,256]{2,1,0:T(8,128)(2,1)S(1)} %get-tuple-element.27), channel_id=1, source_target_pairs={{8,0},{16,8},{24,16},{0,24},{9,1},{17,9},{25,17},{1,25},{10,2},{18... | collective-permute-start | bytes 589832 | tf_op jit(solution)/shard_map/ppermute | solution.py:25
  70.5 6.9 %collective-permute-start.2 = (bf16[24,16,256]{2,1,0:T(8,128)(2,1)S(1)}, bf16[24,16,256]{2,1,0:T(8,128)(2,1)S(1)}, u32[]{:S(2)}, u32[]{:S(2)}) collective-permute-start(bf16[24,16,256]{2,1,0:T(8,128)(2,1)S(1)} %get-tuple-element.28), channel_id=1, source_target_pairs={{0,8},{8,16},{16,24},{24,0},{1,9},{9,17},{17,25},{25,1},{2,10},{10... | collective-permute-start | bytes 589832 | tf_op jit(solution)/shard_map/ppermute | solution.py:24
  80.6 4.2 %copy-start.8 = (pred[2,128]{1,0:T(4,128)(4,1)S(1)}, pred[2,128]{1,0:T(4,128)(4,1)}, u32[]{:S(2)}) copy-start(pred[2,128]{1,0:T(4,128)(4,1)} %broadcast_in_dim.40) | copy-start | bytes 772
  80.6 4.2 %copy-start.10 = (f32[2]{0:T(128)S(1)}, f32[2]{0:T(128)}, u32[]{:S(2)}) copy-start(f32[2]{0:T(128)} %get-tuple-element.36) | copy-start | bytes 28
  160.1 0.8 copy-start
  160.9 0.6 copy-start.4
  161.5 18.1 %copy-start.5 = (bf16[512,128]{1,0:T(8,128)(2,1)S(1)}, bf16[512,128]{1,0:T(8,128)(2,1)}, u32[]{:S(2)}) copy-start(bf16[512,128]{1,0:T(8,128)(2,1)} %copy-done.4) | copy-start | bytes 393220
  161.5 8.4 %collective-permute-start.5 = (bf16[8,64,256]{2,1,0:T(8,128)(2,1)S(1)}, bf16[8,64,256]{2,1,0:T(8,128)(2,1)S(1)}, u32[]{:S(2)}, u32[]{:S(2)}) collective-permute-start(bf16[8,64,256]{2,1,0:T(8,128)(2,1)S(1)} %bitcast.71), channel_id=1, source_target_pairs={{4,0},{5,1},{6,2},{7,3},{12,8},{13,9},{14,10},{15,11},{20,16},{21,... | collective-permute-start | bytes 786440 | tf_op jit(solution)/shard_map/ppermute | solution.py:25
  163.0 8.4 %collective-permute-start.4 = (bf16[8,64,256]{2,1,0:T(8,128)(2,1)S(1)}, bf16[8,64,256]{2,1,0:T(8,128)(2,1)S(1)}, u32[]{:S(2)}, u32[]{:S(2)}) collective-permute-start(bf16[8,64,256]{2,1,0:T(8,128)(2,1)S(1)} %bitcast.72), channel_id=1, source_target_pairs={{0,4},{1,5},{2,6},{3,7},{8,12},{9,13},{10,14},{11,15},{16,20},{17,... | collective-permute-start | bytes 786440 | tf_op jit(solution)/shard_map/ppermute | solution.py:24
  172.2 8.3 %collective-permute-start.7 = (bf16[24,16,256]{2,1,0:T(8,128)(2,1)}, bf16[24,16,256]{2,1,0:T(8,128)(2,1)S(1)}, u32[]{:S(2)}, u32[]{:S(2)}) collective-permute-start(bf16[24,16,256]{2,1,0:T(8,128)(2,1)} %get-tuple-element.23), channel_id=1, source_target_pairs={{8,0},{16,8},{24,16},{0,24},{9,1},{17,9},{25,17},{1,25},{10,2},{18... | collective-permute-start | bytes 589832 | tf_op jit(solution)/shard_map/ppermute | solution.py:25
  172.2 8.3 %collective-permute-start.6 = (bf16[24,16,256]{2,1,0:T(8,128)(2,1)}, bf16[24,16,256]{2,1,0:T(8,128)(2,1)}, u32[]{:S(2)}, u32[]{:S(2)}) collective-permute-start(bf16[24,16,256]{2,1,0:T(8,128)(2,1)} %get-tuple-element.24), channel_id=1, source_target_pairs={{0,8},{8,16},{16,24},{24,0},{1,9},{9,17},{17,25},{25,1},{2,10},{10... | collective-permute-start | bytes 589832 | tf_op jit(solution)/shard_map/ppermute | solution.py:24
  183.3 0.6 copy-start.9
  188.9 1.0 copy-start.1
  188.9 1.1 copy-start.3

commit v2 on v0

v2 whole, which is shorter than its diff:
```python
import jax
import jax.numpy as jnp
from jax import lax
from jax.experimental import pallas as pl
from jax.experimental.pallas import tpu as pltpu
from jax.sharding import PartitionSpec as P

WL = 8
WW = 16
HD = 64
MESH = pl.DeviceIdType.MESH

epsilon = 1e-06


def dot(a, b):
    return jnp.dot(a, b, preferred_element_type=jnp.float32)


def send(src, dst, sems, phase, d, axis, target):
    send_sem, recv_sem = sems
    copy = pltpu.make_async_remote_copy(
        src_ref=src,
        dst_ref=dst,
        send_sem=send_sem.at[phase, d],
        recv_sem=recv_sem.at[phase, d],
        device_id={axis: target},
        device_id_type=MESH,
    )
    copy.start()
    return copy


def ring(axis):
    size = lax.axis_size(axis)
    me = lax.axis_index(axis)
    after = [lax.rem(me + d, size) for d in range(size)]
    before = [lax.rem(me + size - d, size) for d in range(size)]
    return size, me, after, before


def head_unit(x):
    lane = lax.broadcasted_iota(jnp.int32, x.shape, 1)
    square = x * x
    inverse = jnp.zeros_like(x)
    for head in range(x.shape[1] // HD):
        mine = (lane >= head * HD) & (lane < (head + 1) * HD)
        total = jnp.sum(jnp.where(mine, square, 0.0), axis=1, keepdims=True)
        inverse = jnp.where(mine, lax.rsqrt(total + epsilon), inverse)
    return x * inverse


def project_chunk(x, wqkv, q_ref, kv_ref, owner):
    rows, cols = x.shape[0], q_ref.shape[2]
    lon = q_ref.shape[1] - 2 * WW
    per = rows // lon
    projected = dot(x, wqkv)
    lat = pl.ds(WL + owner * per, per)
    inner = slice(WW, WW + lon)
    q_ref[lat, inner, :] = head_unit(projected[:, :cols]).reshape(per, lon, cols)
    keys = head_unit(projected[:, cols : 2 * cols])
    paired = jnp.concatenate([keys, projected[:, 2 * cols :]], axis=1).astype(jnp.bfloat16)
    kv_ref[lat, inner, :] = paired.reshape(per, lon, 2 * cols)


def norm_add(stream, x, gain, bias):
    width = x.shape[1]
    mean = jnp.sum(x, axis=1, keepdims=True) / width
    variance = jnp.sum(x * x, axis=1, keepdims=True) / width - mean * mean
    normed = (x - mean) * lax.rsqrt(variance + 1e-05)
    return (stream.astype(jnp.float32) + gain * normed + bias).astype(jnp.bfloat16)


def gather_project(full, wqkv, q_ref, kv_ref, sems, phase):
    vars_, my_var, to_var, from_var = ring("var")
    outgoing = [
        send(full.at[my_var], full.at[my_var], sems, phase, d, "var", to_var[d])
        for d in range(1, vars_)
    ]
    project_chunk(full[my_var], wqkv, q_ref, kv_ref, my_var)
    for d in range(1, vars_):
        outgoing[d - 1].wait()
        project_chunk(full[from_var[d]], wqkv, q_ref, kv_ref, from_var[d])


def lat_neighbours():
    size, me = lax.axis_size("lat"), lax.axis_index("lat")
    return {1: me < size - 1, -1: me > 0}


def halo(kv_ref, send_sem, recv_sem):
    sects, my_sect = lax.axis_size("sect"), lax.axis_index("sect")
    my_lat = lax.axis_index("lat")
    lon = kv_ref.shape[1] - 2 * WW
    exists = lat_neighbours()
    taken = {0: slice(WW, WW + lon), 1: slice(lon, WW + lon), -1: slice(WW, 2 * WW)}
    placed = {0: slice(WW, WW + lon), 1: slice(0, WW), -1: slice(WW + lon, 2 * WW + lon)}
    landing = {0: slice(WL, 2 * WL), 1: slice(0, WL), -1: slice(2 * WL, 3 * WL)}
    copies = []
    index = 0
    for dl in (1, -1, 0):
        for ds in (0, 1, -1):
            if dl == 0 and ds == 0:
                continue
            target = {"sect": lax.rem(my_sect + ds + sects, sects), "lat": my_lat + dl}
            copy = pltpu.make_async_remote_copy(
                src_ref=kv_ref.at[WL : 2 * WL, taken[ds], :],
                dst_ref=kv_ref.at[landing[dl], placed[ds], :],
                send_sem=send_sem.at[index],
                recv_sem=recv_sem.at[index],
                device_id=target,
                device_id_type=MESH,
            )
            index += 1
            copies.append((dl, copy))
            if dl:
                pl.when(exists[dl])(copy.start)
            else:
                copy.start()
    for dl, copy in copies:
        if dl:
            pl.when(exists[dl])(copy.wait_send)
            pl.when(exists[-dl])(copy.wait_recv)
        else:
            copy.wait()


def attention(layer, shifts, scales, q_ref, kv_ref, wide, q_shifted, kv_shifted, framed, attended):
    lat_rows, lon = WL, q_ref.shape[1] - 2 * WW
    cols = q_ref.shape[2]
    a, b = shifts[layer, 0], shifts[layer, 1]
    my_lat, lats = lax.axis_index("lat"), lax.axis_size("lat")
    wide[...] = kv_ref[...].astype(jnp.float32)
    frame_rows, frame_cols = lat_rows + WL, lon + WW

    def turned(row, step, length):
        return pltpu.roll(row, row.shape[0] - step, 0)[:length].astype(jnp.bfloat16)

    for r in range(frame_rows):
        kv_shifted[r] = turned(wide[a + r], b, frame_cols)
        q_shifted[r] = turned(q_ref[a + r], b, frame_cols)
    lane = lax.broadcasted_iota(jnp.int32, (WL * WW, cols), 1)
    key_row = lax.broadcasted_iota(jnp.int32, (WL * WW, WL * WW), 1) // WW
    heads = cols // HD

    @pl.loop(0, frame_cols // WW)
    def _(n):
        at = pl.ds(pl.multiple_of(n * WW, WW), WW)
        for m in range(frame_rows // WL):
            rows = slice(m * WL, (m + 1) * WL)
            queries = q_shifted[rows, at, :].reshape(WL * WW, cols)
            paired = kv_shifted[rows, at, :].reshape(WL * WW, 2 * cols)
            keys, values = paired[:, :cols], paired[:, cols:]
            place = my_lat * lat_rows - WL + a + m * WL + key_row
            usable = (place >= 0) & (place < lats * lat_rows)
            result = jnp.zeros((WL * WW, cols), jnp.float32)
            for h in range(heads):
                mine = (lane >= h * HD) & (lane < (h + 1) * HD)
                part = jnp.where(mine, queries, jnp.zeros_like(queries))
                scores = lax.dot_general(
                    part, keys, (((1,), (1,)), ((), ())), preferred_element_type=jnp.float32
                )
                scale = scales[layer, h]
                expo = jnp.where(usable, jnp.exp((scores - 1.0) * scale), 0.0)
                total = jnp.sum(expo, axis=1, keepdims=True)
                weights = (expo / total).astype(jnp.bfloat16)
                result = jnp.where(mine, dot(weights, values), result)
            framed[rows, at, :] = result.reshape(WL, WW, cols)

    for r in range(lat_rows):
        attended[r * lon : (r + 1) * lon, :] = turned(framed[WL - a + r], WW - b, lon)


def feed(
    layer, attended, wout, x_ref, params, w_in, w_out, part, part_in, mid, back, back_in, full, sems
):
    vars_, my_var, to_var, from_var = ring("var")
    rows = mid.shape[1]

    def chosen(kind, position):
        index = (kind * 2 + layer) * 2 + position
        return jnp.concatenate([params[v, index : index + 1, :] for v in range(vars_)], axis=1)

    def mixed_of(owner):
        at = pl.ds(pl.multiple_of(owner * rows, rows), rows)
        return dot(attended[at, :], wout[layer])

    def fed_of(x):
        hidden = jax.nn.gelu(dot(x, w_in[layer]), approximate=True).astype(jnp.bfloat16)
        return dot(hidden, w_out[layer])

    first = 4 + 4 * layer
    outgoing = []
    for d in range(1, vars_):
        part[d - 1] = mixed_of(to_var[d]).astype(jnp.bfloat16)
        outgoing.append(send(part.at[d - 1], part_in.at[d - 1], sems, first, d, "var", to_var[d]))
    total = mixed_of(my_var)
    for d in range(1, vars_):
        outgoing[d - 1].wait()
        total = total + part_in[d - 1].astype(jnp.float32)
    mid[my_var] = norm_add(x_ref[my_var], total, chosen(0, 0), chosen(1, 0))
    outgoing = [
        send(mid.at[my_var], mid.at[my_var], sems, first + 1, d, "var", to_var[d])
        for d in range(1, vars_)
    ]
    total = fed_of(mid[my_var])
    returned = []
    for d in range(1, vars_):
        outgoing[d - 1].wait()
        back[d - 1] = fed_of(mid[from_var[d]]).astype(jnp.bfloat16)
        returned.append(
            send(back.at[d - 1], back_in.at[d - 1], sems, first + 2, d, "var", from_var[d])
        )
    for d in range(1, vars_):
        returned[d - 1].wait()
        total = total + back_in[d - 1].astype(jnp.float32)
    full[my_var] = norm_add(mid[my_var], total, chosen(0, 1), chosen(1, 1))


def whole_kernel(
    patches, table, wqkv, wout, w_in, w_out, scales, params, decode, shifts, out_ref,
    patch_in, table_in, params_in, part, part_in, full, mid, back, back_in,
    q_ref, kv_ref, wide, q_shifted, kv_shifted, framed, attended,
    decode_in, made, landed, send_sem, recv_sem, halo_send, halo_recv,
):
    sems = (send_sem, recv_sem)
    sects, my_sect, to_sect, from_sect = ring("sect")
    vars_, my_var, to_var, from_var = ring("var")
    layers = wqkv.shape[0]
    lat_rows, lon_total, depth = patches.shape
    cols = lon_total // sects
    rows = full.shape[2]
    per = rows // cols
    for layer in range(layers):
        kv_ref[layer, :WL] = jnp.zeros_like(kv_ref[layer, :WL])
        kv_ref[layer, 2 * WL :] = jnp.zeros_like(kv_ref[layer, 2 * WL :])
    q_ref[...] = jnp.zeros_like(q_ref)
    exists = lat_neighbours()
    barrier = pltpu.get_barrier_semaphore()
    my_lat = lax.axis_index("lat")
    for dl in (1, -1):
        @pl.when(exists[dl])
        def _():
            for ds in (0, 1, -1):
                target = {"sect": lax.rem(my_sect + ds + sects, sects), "lat": my_lat + dl}
                pl.semaphore_signal(barrier, inc=1, device_id=target, device_id_type=MESH)
    around = exists[1].astype(jnp.int32) + exists[-1].astype(jnp.int32)
    for axis, size, me in (("sect", sects, my_sect), ("var", vars_, my_var)):
        for d in range(1, size):
            pl.semaphore_signal(
                barrier, inc=1, device_id={axis: lax.rem(me + d, size)}, device_id_type=MESH
            )
    pl.semaphore_wait(barrier, sects + vars_ - 2 + 3 * around)

    last = 4 + 4 * layers
    moved, later = [], []
    for d in range(1, sects):
        t = to_sect[d]
        moved.append(send(table, table_in.at[d - 1], sems, 0, d, "sect", t))
        moved.append(
            send(
                patches.at[:, pl.ds(pl.multiple_of(t * cols, cols), cols), :],
                patch_in.at[d - 1], sems, 1, d, "sect", t,
            )
        )
    params_in[my_var] = params[...]
    for d in range(1, vars_):
        later.append(send(params, params_in.at[my_var], sems, 2, d, "var", to_var[d]))
    for copy in moved:
        copy.wait()
    weights = jnp.concatenate([table[...]] + [table_in[d] for d in range(sects - 1)], axis=0)

    def partial_of(owner):
        lat = pl.ds(owner * per, per)
        own = patches[lat, pl.ds(pl.multiple_of(my_sect * cols, cols), cols), :]
        blocks = [own] + [patch_in[d, lat] for d in range(sects - 1)]
        x = jnp.concatenate([block.reshape(rows, depth) for block in blocks], axis=1)
        return dot(x, weights)

    outgoing = []
    for d in range(1, vars_):
        part[layers, d - 1] = partial_of(to_var[d]).astype(jnp.bfloat16)
        outgoing.append(
            send(part.at[layers, d - 1], part_in.at[layers, d - 1], sems, 3, d, "var", to_var[d])
        )
    total = partial_of(my_var)
    for d in range(1, vars_):
        outgoing[d - 1].wait()
        total = total + part_in[layers, d - 1].astype(jnp.float32)
    full[0, my_var] = total.astype(jnp.bfloat16)
    for d in range(1, sects):
        later.append(send(decode, decode_in.at[d - 1], sems, last, d, "sect", to_sect[d]))
    for layer in range(layers):
        gather_project(
            full.at[layer], wqkv[layer], q_ref, kv_ref.at[layer], sems, 7 + 4 * layer
        )
        if layer == 0:
            for copy in later:
                copy.wait()
        halo(kv_ref.at[layer], halo_send.at[layer], halo_recv.at[layer])
        attention(
            layer, shifts, scales, q_ref, kv_ref.at[layer], wide, q_shifted, kv_shifted,
            framed, attended,
        )
        feed(
            layer, attended, wout, full.at[layer], params_in, w_in, w_out,
            part.at[layer], part_in.at[layer], mid.at[layer], back.at[layer], back_in.at[layer],
            full.at[layer + 1], sems,
        )
    stream = full.at[layers]
    outgoing = [
        send(stream.at[my_var], stream.at[my_var], sems, last + 1, d, "var", to_var[d])
        for d in range(1, vars_)
    ]
    weights = jnp.concatenate([decode[...]] + [decode_in[d] for d in range(sects - 1)], axis=1)
    copies = []
    for k in range(vars_):
        if k:
            outgoing[k - 1].wait()
        lat = pl.ds(from_var[k] * per, per)
        decoded = dot(stream[from_var[k]], weights).astype(jnp.bfloat16)
        for d in range(sects):
            block = decoded[:, d * depth : (d + 1) * depth].reshape(per, cols, depth)
            made[d, lat] = block
            if d:
                copies.append(
                    send(
                        made.at[d, lat], landed.at[sects - d, lat], sems, last + 2 + k, d, "sect",
                        from_sect[d],
                    )
                )
    out_ref[:, pl.ds(pl.multiple_of(my_sect * cols, cols), cols), :] = made[0]
    for copy in copies:
        copy.wait()
    for d in range(1, sects):
        at = pl.ds(pl.multiple_of(to_sect[d] * cols, cols), cols)
        out_ref[:, at, :] = landed[sects - d]


def per_device(
    patches,
    embed_weight,
    qkv_weight,
    out_weight,
    mlp_in_weight,
    mlp_out_weight,
    logit_scale,
    norm_gain,
    norm_bias,
    decode_weight,
    shifts,
):
    _, lat_rows, lon_total, patch_dim = patches.shape
    width = embed_weight.shape[2]
    layers, _, _, head_cols = qkv_weight.shape
    sects, vars_ = lax.axis_size("sect"), lax.axis_size("var")
    cols = lon_total // sects
    tokens = lat_rows * cols
    rows = tokens // vars_
    bf = jnp.bfloat16
    vmem = pl.BlockSpec(memory_space=pltpu.VMEM)
    smem = pl.BlockSpec(memory_space=pltpu.SMEM)
    wqkv = qkv_weight.reshape(layers, width, 3 * head_cols)
    params = jnp.concatenate(
        [norm_gain.reshape(2 * layers, -1), norm_bias.reshape(2 * layers, -1)], axis=0
    )
    shards = pltpu.VMEM((layers + 1, vars_ - 1, rows, width), bf)
    ext_rows, ext_cols = lat_rows + 2 * WL, cols + 2 * WW
    phases = 4 + 4 * layers + 2 + vars_
    scratch = [
        pltpu.VMEM((sects - 1, lat_rows, cols, patch_dim), bf),
        pltpu.VMEM((sects - 1, patch_dim, width), bf),
        pltpu.VMEM((vars_,) + params.shape, jnp.float32),
        shards,
        shards,
        pltpu.VMEM((layers + 1, vars_, rows, width), bf),
        pltpu.VMEM((layers, vars_, rows, width), bf),
        shards,
        shards,
        pltpu.VMEM((ext_rows, ext_cols, head_cols), jnp.float32),
        pltpu.VMEM((layers, ext_rows, ext_cols, 2 * head_cols), bf),
        pltpu.VMEM((ext_rows, ext_cols, 2 * head_cols), jnp.float32),
        pltpu.VMEM((lat_rows + WL, cols + WW, head_cols), bf),
        pltpu.VMEM((lat_rows + WL, cols + WW, 2 * head_cols), bf),
        pltpu.VMEM((lat_rows + WL, cols + WW, head_cols), jnp.float32),
        pltpu.VMEM((tokens, head_cols), bf),
        pltpu.VMEM((sects - 1, width, patch_dim), bf),
        pltpu.VMEM((sects, lat_rows, cols, patch_dim), bf),
        pltpu.VMEM((sects, lat_rows, cols, patch_dim), bf),
        pltpu.SemaphoreType.DMA((phases, 4)),
        pltpu.SemaphoreType.DMA((phases, 4)),
        pltpu.SemaphoreType.DMA((layers, 8)),
        pltpu.SemaphoreType.DMA((layers, 8)),
    ]
    out = pl.pallas_call(
        whole_kernel,
        out_shape=jax.ShapeDtypeStruct((lat_rows, lon_total, patch_dim), bf),
        in_specs=[vmem] * 6 + [smem] + [vmem] * 2 + [smem],
        out_specs=vmem,
        scratch_shapes=scratch,
        compiler_params=pltpu.CompilerParams(
            collective_id=0, has_side_effects=True, vmem_limit_bytes=48 * 1024 * 1024
        ),
    )(
        patches[0], embed_weight[0], wqkv, out_weight, mlp_in_weight, mlp_out_weight,
        logit_scale, params, decode_weight[0], shifts,
    )
    return out[None]


def solution(mesh):
    return jax.shard_map(
        per_device,
        mesh=mesh,
        in_specs=(
            P(("sect", "var"), "lat", None, None),
            P(("sect", "var"), None, None),
            P(None, None, None, "var"),
            P(None, "var", None),
            P(None, None, "var"),
            P(None, "var", None),
            P(None, "var"),
            P(None, None, "var"),
            P(None, None, "var"),
            P(("sect", "var"), None, None),
            P(),
        ),
        out_specs=P(("sect", "var"), "lat", None, None),
        check_vma=False,
    )
```

time: 412 us -> 193 us (0.47)
  waiting for transfers between devices: 210 us -> 0 us
  Pallas kernels: 0 us -> 184 us
  blocking collectives: 109 us -> 0 us
  between operations: 28.2 us -> 0.08 us
  other arithmetic: 17.5 us -> 0.01 us
  matrix products: 14.6 us -> 0 us
  starting transfers between devices: 13 us -> 0 us
  local copies, waits for them, and re-layouts: 18.4 us -> 7.96 us
    pallas_call x0 -> x1, Pallas kernels: none -> 184 us  [per_device(): pl.pallas_call(whole_kernel, out_shape=jax.ShapeDtypeStruct((lat_rows, lo...]
    reduce_scatter x5 -> x0, waiting for transfers between devices: 181 us -> none  [the longest x1 73.2 us: per_device(): lax.psum_scatter(partial_value, ('sect', 'var'), scatter_dimension=1, til...]
    all_gather x5 -> x0, blocking collectives: 70.9 us -> none  [the longest x2 28.6 us: layer_heads(): gathered = lax.all_gather(stream, 'var', axis=2, tiled=True)]
    psum x4 -> x0, blocking collectives: 38.2 us -> none  [the longest x2 19.1 us: layer_heads(): lax.psum((jnp.sum(mixed_sum, axis=-1), jnp.sum(mixed_sum * mixed_sum, axi...]
    all_gather x1 -> x0, waiting for transfers between devices: 21.8 us -> none  [per_device(): lax.all_gather(gathered, 'sect', axis=1, tiled=True)]
    dot_general x12 -> x0, matrix products: 13.2 us -> none  [the longest x2 3.78 us: layer_heads(): jnp.einsum('rlf,fd->rld', hidden, w_out, preferred_element_type=jnp.float32)]
    ppermute x8 -> x0, starting transfers between devices: 12.8 us -> none  [the longest x4 6.69 us: extended(): before = lax.ppermute(last, axis, up)]
    ppermute x8 -> x0, waiting for transfers between devices: 7.56 us -> none  [the longest x4 6.26 us: extended(): before = lax.ppermute(last, axis, up)]
  transfers between devices with their start and end apart: 14 -> 0, of which waited for: 10 -> 0; matrix products, arithmetic and copies ran while one was open for 2% -> 0% of each run, Pallas kernels for 0% -> 0%
where the time goes in v2:
time: 193 us; the launch traced here: 192 us
  Pallas kernels  184 us (95%)
  local copies, waits for them, and re-layouts  7.96 us (4%)
    pallas_call x1, Pallas kernels, per_device(): pl.pallas_call(whole_kernel, out_shape=jax.ShapeDtypeStruct((lat_rows, lo...  184 us
    unnamed x22, local copies, waits for them, and re-layouts  6.35 us

profile of v2, /device:TPU:0, one launch (start us, length us, event | category | flops | bytes accessed | tf_op | source)
XLA Modules:
  0.0 192.1 jit_solution(14240447763811120061)
XLA Ops:
  0.0 0.0 copy-start.1
  0.0 0.0 copy-start.4
  0.0 2.4 %copy.13 = bf16[2,512,3,128]{1,3,2,0:T(8,128)(2,1)} copy(bf16[2,512,3,128]{3,1,2,0:T(8,128)(2,1)} %param.13) | data formatting | bytes 1572864 | tf_op args[2]
  2.4 0.0 copy-start
  2.4 0.0 copy-start.9
  2.4 0.0 copy-start.2
  2.4 0.0 copy-start.7
  2.4 1.6 copy.14.wqkv
  4.0 0.0 copy-start.8
  4.0 0.0 copy-done.9
  4.0 0.7 copy-done.8
  4.7 0.0 copy-start.6
  4.7 0.0 copy-done.1
  4.7 0.0 copy-done.4
  4.7 0.0 copy-done
  4.7 0.0 copy-done.2
  4.8 0.0 copy-done.7
  4.8 0.6 copy-done.6
  5.4 0.0 copy-start.3
  5.4 0.9 copy-done.3
  6.3 0.0 copy-start.5
  6.3 0.9 copy-done.5
  7.2 184.1 %shard_map.109 = bf16[8,256,128]{2,1,0:T(8,128)(2,1)S(1)} custom-call(bf16[8,256,128]{2,1,0:T(8,128)(2,1)S(1)} %bitcast.8, bf16[128,512]{1,0:T(8,128)(2,1)S(1)} %bitcast.9, bf16[2,512,384]{2,1,0:T(8,128)(2,1)S(1)} %copy.14.wqkv, bf16[2,128,512]{2,1,0:T(8,128)(2,1)S(1)} %copy-done.3, bf16[2,512,512]{2,1,0:T(8,128)(2,1)S(1)} %copy-done, ...), custom_call_target="tpu_custom_call" | custom-call | tf_op jit(solution)/shard_map/pallas_call | solution.py:395
  191.3 0.8 copy.16
  (1 shorter events, 0.0 us)
Async XLA Ops:
  0.0 4.7 %copy-start.1 = (bf16[2,512,512]{2,1,0:T(8,128)(2,1)S(1)}, bf16[2,512,512]{2,1,0:T(8,128)(2,1)}, u32[]{:S(2)}) copy-start(bf16[2,512,512]{2,1,0:T(8,128)(2,1)} %w_out.1) | copy-start | bytes 3145732
  0.0 4.7 %copy-start.4 = (bf16[1,128,512]{2,1,0:T(8,128)(2,1)S(1)}, bf16[1,128,512]{2,1,0:T(8,128)(2,1)}, u32[]{:S(2)}) copy-start(bf16[1,128,512]{2,1,0:T(8,128)(2,1)} %param.12) | copy-start | bytes 393220
  2.4 2.3 %copy-start = (bf16[2,512,512]{2,1,0:T(8,128)(2,1)S(1)}, bf16[2,512,512]{2,1,0:T(8,128)(2,1)}, u32[]{:S(2)}) copy-start(bf16[2,512,512]{2,1,0:T(8,128)(2,1)} %w_in.1) | copy-start | bytes 3145732
  2.4 1.6 copy-start.9
  2.4 2.4 %copy-start.2 = (bf16[1,8,256,128]{3,2,1,0:T(8,128)(2,1)S(1)}, bf16[1,8,256,128]{3,2,1,0:T(8,128)(2,1)}, u32[]{:S(2)}) copy-start(bf16[1,8,256,128]{3,2,1,0:T(8,128)(2,1)} %param.11) | copy-start | bytes 1572868
  2.4 2.4 %copy-start.7 = (s32[2,2]{1,0:T(2,128)S(1)}, s32[2,2]{1,0:T(2,128)}, u32[]{:S(2)}) copy-start(s32[2,2]{1,0:T(2,128)} %shifts.1) | copy-start | bytes 52
  4.0 0.7 copy-start.8
  4.7 0.7 copy-start.6
  5.4 0.9 copy-start.3
  6.3 0.9 copy-start.5

commit v3 on v2

--- a/solution.py
+++ b/solution.py
@@ -171,57 +171,99 @@
         attended[r * lon : (r + 1) * lon, :] = turned(framed[WL - a + r], WW - b, lon)
 
 
-def feed(
-    layer, attended, wout, x_ref, params, w_in, w_out, part, part_in, mid, back, back_in, full, sems
-):
+def pieces(stack_rows):
+    sect, lat = lax.axis_index("sect"), lax.axis_index("lat")
+    core, across, pair = lax.rem(sect, 2), sect // 2, lax.rem(lat, 2)
+    step = stack_rows // 8
+    own = (core * 2 + across) * 2 + pair
+    ranges = [(own, 1), (core * 2 + across, 2), (core, 4)]
+    targets = [
+        {"lat": lat + 1 - 2 * pair},
+        {"sect": sect + 2 - 4 * across},
+        {"sect": sect + 1 - 2 * core},
+    ]
+    at = [
+        pl.ds(pl.multiple_of(index * (count * step), 16), count * step) for index, count in ranges
+    ]
+    return at, targets
+
+
+def spread(stack, others, send_sem, recv_sem):
     vars_, my_var, to_var, from_var = ring("var")
-    rows = mid.shape[1]
+    at, targets = pieces(stack.shape[0])
+    groups = [
+        [
+            pltpu.make_async_remote_copy(
+                src_ref=stack.at[at[0]],
+                dst_ref=others.at[d - 1, at[0]],
+                send_sem=send_sem.at[d - 1],
+                recv_sem=recv_sem.at[d - 1],
+                device_id={"var": to_var[d]},
+                device_id_type=MESH,
+            )
+            for d in range(1, vars_)
+        ]
+    ]
+    for k in range(3):
+        groups.append(
+            [
+                pltpu.make_async_remote_copy(
+                    src_ref=others.at[:, at[k]],
+                    dst_ref=others.at[:, at[k]],
+                    send_sem=send_sem.at[vars_ - 1 + k],
+                    recv_sem=recv_sem.at[vars_ - 1 + k],
+                    device_id=targets[k],
+                    device_id_type=MESH,
+                )
+            ]
+        )
+    return groups
+
+
+def advance(groups, stage):
+    if stage:
+        for copy in groups[stage - 1]:
+            copy.wait()
+    if stage < len(groups):
+        for copy in groups[stage]:
+            copy.start()
+
+
+def feed(layer, attended, attended_in, stack, others, params, x_ref, out_ref, sems, phase):
+    vars_, my_var, to_var, from_var = ring("var")
+    rows, heads_part = attended_in.shape[1:]
+    width = x_ref.shape[2]
 
     def chosen(kind, position):
         index = (kind * 2 + layer) * 2 + position
         return jnp.concatenate([params[v, index : index + 1, :] for v in range(vars_)], axis=1)
 
-    def mixed_of(owner):
-        at = pl.ds(pl.multiple_of(owner * rows, rows), rows)
-        return dot(attended[at, :], wout[layer])
-
-    def fed_of(x):
-        hidden = jax.nn.gelu(dot(x, w_in[layer]), approximate=True).astype(jnp.bfloat16)
-        return dot(hidden, w_out[layer])
-
-    first = 4 + 4 * layer
     outgoing = []
     for d in range(1, vars_):
-        part[d - 1] = mixed_of(to_var[d]).astype(jnp.bfloat16)
-        outgoing.append(send(part.at[d - 1], part_in.at[d - 1], sems, first, d, "var", to_var[d]))
-    total = mixed_of(my_var)
+        at = pl.ds(pl.multiple_of(to_var[d] * rows, rows), rows)
+        outgoing.append(
+            send(attended.at[at], attended_in.at[d - 1], sems, phase, d, "var", to_var[d])
+        )
+    own = attended[pl.ds(pl.multiple_of(my_var * rows, rows), rows), :]
+    total = dot(own, stack[:heads_part])
     for d in range(1, vars_):
         outgoing[d - 1].wait()
-        total = total + part_in[d - 1].astype(jnp.float32)
-    mid[my_var] = norm_add(x_ref[my_var], total, chosen(0, 0), chosen(1, 0))
-    outgoing = [
-        send(mid.at[my_var], mid.at[my_var], sems, first + 1, d, "var", to_var[d])
-        for d in range(1, vars_)
-    ]
-    total = fed_of(mid[my_var])
-    returned = []
-    for d in range(1, vars_):
-        outgoing[d - 1].wait()
-        back[d - 1] = fed_of(mid[from_var[d]]).astype(jnp.bfloat16)
-        returned.append(
-            send(back.at[d - 1], back_in.at[d - 1], sems, first + 2, d, "var", from_var[d])
-        )
-    for d in range(1, vars_):
-        returned[d - 1].wait()
-        total = total + back_in[d - 1].astype(jnp.float32)
-    full[my_var] = norm_add(mid[my_var], total, chosen(0, 1), chosen(1, 1))
+        total = total + dot(attended_in[d - 1], others[d - 1, :heads_part])
+    mid = norm_add(x_ref[my_var], total, chosen(0, 0), chosen(1, 0))
+    first = slice(heads_part, heads_part + width)
+    total = jnp.zeros((rows, width), jnp.float32)
+    for d in range(vars_):
+        shard = stack if d == 0 else others.at[d - 1]
+        hidden = jax.nn.gelu(dot(mid, shard[first]), approximate=True).astype(jnp.bfloat16)
+        total = total + dot(hidden, shard[heads_part + width :])
+    out_ref[my_var] = norm_add(mid, total, chosen(0, 1), chosen(1, 1))
 
 
 def whole_kernel(
-    patches, table, wqkv, wout, w_in, w_out, scales, params, decode, shifts, out_ref,
-    patch_in, table_in, params_in, part, part_in, full, mid, back, back_in,
+    patches, table, wqkv, stack, scales, params, decode, shifts, out_ref,
+    patch_in, table_in, params_in, part, part_in, full, others, attended_in,
     q_ref, kv_ref, wide, q_shifted, kv_shifted, framed, attended,
-    decode_in, made, landed, send_sem, recv_sem, halo_send, halo_recv,
+    decode_in, made, landed, send_sem, recv_sem, halo_send, halo_recv, spread_send, spread_recv,
 ):
     sems = (send_sem, recv_sem)
     sects, my_sect, to_sect, from_sect = ring("sect")
@@ -266,6 +308,11 @@
     params_in[my_var] = params[...]
     for d in range(1, vars_):
         later.append(send(params, params_in.at[my_var], sems, 2, d, "var", to_var[d]))
+    carried = [
+        spread(stack.at[layer], others.at[layer], spread_send.at[layer], spread_recv.at[layer])
+        for layer in range(layers)
+    ]
+    advance(carried[0], 0)
     for copy in moved:
         copy.wait()
     weights = jnp.concatenate([table[...]] + [table_in[d] for d in range(sects - 1)], axis=0)
@@ -279,17 +326,19 @@
 
     outgoing = []
     for d in range(1, vars_):
-        part[layers, d - 1] = partial_of(to_var[d]).astype(jnp.bfloat16)
+        part[d - 1] = partial_of(to_var[d]).astype(jnp.bfloat16)
         outgoing.append(
-            send(part.at[layers, d - 1], part_in.at[layers, d - 1], sems, 3, d, "var", to_var[d])
-        )
+            send(part.at[d - 1], part_in.at[d - 1], sems, 3, d, "var", to_var[d])
+        )
+    advance(carried[0], 1)
     total = partial_of(my_var)
     for d in range(1, vars_):
         outgoing[d - 1].wait()
-        total = total + part_in[layers, d - 1].astype(jnp.float32)
+        total = total + part_in[d - 1].astype(jnp.float32)
     full[0, my_var] = total.astype(jnp.bfloat16)
     for d in range(1, sects):
         later.append(send(decode, decode_in.at[d - 1], sems, last, d, "sect", to_sect[d]))
+    advance(carried[0], 2)
     for layer in range(layers):
         gather_project(
             full.at[layer], wqkv[layer], q_ref, kv_ref.at[layer], sems, 7 + 4 * layer
@@ -297,16 +346,23 @@
         if layer == 0:
             for copy in later:
                 copy.wait()
+        advance(carried[layer], 3)
+        if layer + 1 < layers:
+            advance(carried[layer + 1], 0)
         halo(kv_ref.at[layer], halo_send.at[layer], halo_recv.at[layer])
         attention(
             layer, shifts, scales, q_ref, kv_ref.at[layer], wide, q_shifted, kv_shifted,
-            framed, attended,
-        )
+            framed, attended.at[layer],
+        )
+        advance(carried[layer], 4)
+        if layer + 1 < layers:
+            advance(carried[layer + 1], 1)
         feed(
-            layer, attended, wout, full.at[layer], params_in, w_in, w_out,
-            part.at[layer], part_in.at[layer], mid.at[layer], back.at[layer], back_in.at[layer],
-            full.at[layer + 1], sems,
-        )
+            layer, attended.at[layer], attended_in.at[layer], stack.at[layer], others.at[layer],
+            params_in, full.at[layer], full.at[layer + 1], sems, 4 + 4 * layer,
+        )
+        if layer + 1 < layers:
+            advance(carried[layer + 1], 2)
     stream = full.at[layers]
     outgoing = [
         send(stream.at[my_var], stream.at[my_var], sems, last + 1, d, "var", to_var[d])
@@ -364,7 +420,8 @@
     params = jnp.concatenate(
         [norm_gain.reshape(2 * layers, -1), norm_bias.reshape(2 * layers, -1)], axis=0
     )
-    shards = pltpu.VMEM((layers + 1, vars_ - 1, rows, width), bf)
+    stack = jnp.concatenate([out_weight, mlp_in_weight, mlp_out_weight], axis=1)
+    shards = pltpu.VMEM((vars_ - 1, rows, width), bf)
     ext_rows, ext_cols = lat_rows + 2 * WL, cols + 2 * WW
     phases = 4 + 4 * layers + 2 + vars_
     scratch = [
@@ -374,16 +431,15 @@
         shards,
         shards,
         pltpu.VMEM((layers + 1, vars_, rows, width), bf),
-        pltpu.VMEM((layers, vars_, rows, width), bf),
-        shards,
-        shards,
+        pltpu.VMEM((layers, vars_ - 1) + stack.shape[1:], bf),
+        pltpu.VMEM((layers, vars_ - 1, rows, head_cols), bf),
         pltpu.VMEM((ext_rows, ext_cols, head_cols), jnp.float32),
         pltpu.VMEM((layers, ext_rows, ext_cols, 2 * head_cols), bf),
         pltpu.VMEM((ext_rows, ext_cols, 2 * head_cols), jnp.float32),
         pltpu.VMEM((lat_rows + WL, cols + WW, head_cols), bf),
         pltpu.VMEM((lat_rows + WL, cols + WW, 2 * head_cols), bf),
         pltpu.VMEM((lat_rows + WL, cols + WW, head_cols), jnp.float32),
-        pltpu.VMEM((tokens, head_cols), bf),
+        pltpu.VMEM((layers, tokens, head_cols), bf),
         pltpu.VMEM((sects - 1, width, patch_dim), bf),
         pltpu.VMEM((sects, lat_rows, cols, patch_dim), bf),
         pltpu.VMEM((sects, lat_rows, cols, patch_dim), bf),
@@ -391,18 +447,20 @@
         pltpu.SemaphoreType.DMA((phases, 4)),
         pltpu.SemaphoreType.DMA((layers, 8)),
         pltpu.SemaphoreType.DMA((layers, 8)),
+        pltpu.SemaphoreType.DMA((layers, vars_ + 2)),
+        pltpu.SemaphoreType.DMA((layers, vars_ + 2)),
     ]
     out = pl.pallas_call(
         whole_kernel,
         out_shape=jax.ShapeDtypeStruct((lat_rows, lon_total, patch_dim), bf),
-        in_specs=[vmem] * 6 + [smem] + [vmem] * 2 + [smem],
+        in_specs=[vmem] * 4 + [smem] + [vmem] * 2 + [smem],
         out_specs=vmem,
         scratch_shapes=scratch,
         compiler_params=pltpu.CompilerParams(
             collective_id=0, has_side_effects=True, vmem_limit_bytes=48 * 1024 * 1024
         ),
     )(
-        patches[0], embed_weight[0], wqkv, out_weight, mlp_in_weight, mlp_out_weight,
+        patches[0], embed_weight[0], wqkv, stack,
         logit_scale, params, decode_weight[0], shifts,
     )
     return out[None]

time: 193 us -> 150 us (0.78)
  Pallas kernels: 184 us -> 145 us
  local copies, waits for them, and re-layouts: 7.96 us -> 2.59 us
  other arithmetic: 0.01 us -> 2.25 us
    pallas_call x1, Pallas kernels: 184 us -> 145 us  [per_device(): pl.pallas_call(whole_kernel, out_shape=jax.ShapeDtypeStruct((lat_rows, lo...]
    unnamed x22 -> x16, local copies, waits for them, and re-layouts: 6.35 us -> 2.24 us
where the time goes in v3:
time: 150 us
  Pallas kernels  145 us (97%)
  local copies, waits for them, and re-layouts  2.59 us (2%)
  other arithmetic  2.25 us (2%)
    pallas_call x1, Pallas kernels, per_device(): pl.pallas_call(whole_kernel, out_shape=jax.ShapeDtypeStruct((lat_rows, lo...  145 us

profile of v3, /device:TPU:0, one launch (start us, length us, event | category | flops | bytes accessed | tf_op | source)
XLA Modules:
  0.0 150.3 jit_solution(5117465897483657335)
XLA Ops:
  0.0 0.0 copy-start.5
  0.0 0.0 copy-start.6
  0.0 0.8 pad_maximum_fusion.1.params
  0.8 1.4 copy.13
  2.2 0.4 copy.14.wqkv
  2.6 0.0 copy-done.5
  2.6 0.0 copy-done.6
  2.6 0.0 copy-start
  2.6 0.0 copy-start.1
  2.6 0.0 copy-start.2
  2.6 0.0 copy-start.3
  2.7 0.0 copy-start.4
  2.7 1.4 pad_maximum_fusion.stack
  4.1 0.0 copy-done
  4.1 0.0 copy-done.1
  4.1 0.0 copy-done.2
  4.1 0.0 copy-done.3
  4.2 0.0 copy-done.4
  4.2 145.3 %shard_map.109 = bf16[8,256,128]{2,1,0:T(8,128)(2,1)S(1)} custom-call(bf16[8,256,128]{2,1,0:T(8,128)(2,1)S(1)} %bitcast.8, bf16[128,512]{1,0:T(8,128)(2,1)S(1)} %bitcast.9, bf16[2,512,384]{2,1,0:T(8,128)(2,1)S(1)} %copy.14.wqkv, bf16[2,1152,512]{2,1,0:T(8,128)(2,1)S(1)} %pad_maximum_fusion.stack, f32[2,2]{1,0:T(2,128)S(1)} %copy-done.3, ...), custom_call_target="tpu_custom_call" | custom-call | tf_op jit(solution)/shard_map/pallas_call | solution.py:453
  149.5 0.8 copy.16
Async XLA Ops:
  0.0 2.6 %copy-start.5 = (bf16[2,512,512]{2,1,0:T(8,128)(2,1)S(1)}, bf16[2,512,512]{2,1,0:T(8,128)(2,1)}, u32[]{:S(2)}) copy-start(bf16[2,512,512]{2,1,0:T(8,128)(2,1)} %param.16) | copy-start | bytes 3145732
  0.0 2.6 %copy-start.6 = (bf16[2,128,512]{2,1,0:T(8,128)(2,1)S(1)}, bf16[2,128,512]{2,1,0:T(8,128)(2,1)}, u32[]{:S(2)}) copy-start(bf16[2,128,512]{2,1,0:T(8,128)(2,1)} %param.14) | copy-start | bytes 786436
  2.6 1.5 %copy-start = (bf16[1,8,256,128]{3,2,1,0:T(8,128)(2,1)S(1)}, bf16[1,8,256,128]{3,2,1,0:T(8,128)(2,1)}, u32[]{:S(2)}) copy-start(bf16[1,8,256,128]{3,2,1,0:T(8,128)(2,1)} %param.11) | copy-start | bytes 1572868
  2.6 1.5 %copy-start.1 = (bf16[1,128,512]{2,1,0:T(8,128)(2,1)S(1)}, bf16[1,128,512]{2,1,0:T(8,128)(2,1)}, u32[]{:S(2)}) copy-start(bf16[1,128,512]{2,1,0:T(8,128)(2,1)} %param.12) | copy-start | bytes 393220
  2.6 1.5 %copy-start.2 = (bf16[1,512,128]{2,1,0:T(8,128)(2,1)S(1)}, bf16[1,512,128]{2,1,0:T(8,128)(2,1)}, u32[]{:S(2)}) copy-start(bf16[1,512,128]{2,1,0:T(8,128)(2,1)} %param.20) | copy-start | bytes 393220
  2.6 1.5 %copy-start.3 = (f32[2,2]{1,0:T(2,128)S(1)}, f32[2,2]{1,0:T(2,128)}, u32[]{:S(2)}) copy-start(f32[2,2]{1,0:T(2,128)} %scales.1) | copy-start | bytes 52
  2.7 1.5 copy-start.4

commit v4 on v3

--- a/solution.py
+++ b/solution.py
@@ -54,7 +54,7 @@
     rows, cols = x.shape[0], q_ref.shape[2]
     lon = q_ref.shape[1] - 2 * WW
     per = rows // lon
-    projected = dot(x, wqkv)
+    projected = dot(x, jnp.concatenate([wqkv[i] for i in range(3)], axis=1))
     lat = pl.ds(WL + owner * per, per)
     inner = slice(WW, WW + lon)
     q_ref[lat, inner, :] = head_unit(projected[:, :cols]).reshape(per, lon, cols)
@@ -71,16 +71,26 @@
     return (stream.astype(jnp.float32) + gain * normed + bias).astype(jnp.bfloat16)
 
 
-def gather_project(full, wqkv, q_ref, kv_ref, sems, phase):
+def gather_project(full, wqkv, q_ref, kv_ref, sems, phase, halo_sems):
     vars_, my_var, to_var, from_var = ring("var")
     outgoing = [
         send(full.at[my_var], full.at[my_var], sems, phase, d, "var", to_var[d])
         for d in range(1, vars_)
     ]
-    project_chunk(full[my_var], wqkv, q_ref, kv_ref, my_var)
-    for d in range(1, vars_):
-        outgoing[d - 1].wait()
+    per = full.shape[1] // (kv_ref.shape[1] - 2 * WW)
+    copies = []
+    for d in range(vars_):
+        if d:
+            outgoing[d - 1].wait()
         project_chunk(full[from_var[d]], wqkv, q_ref, kv_ref, from_var[d])
+        copies += halo(kv_ref, from_var[d] * per, per, halo_sems, d)
+    exists = lat_neighbours()
+    for dl, copy in copies:
+        if dl:
+            pl.when(exists[dl])(copy.wait_send)
+            pl.when(exists[-dl])(copy.wait_recv)
+        else:
+            copy.wait()
 
 
 def lat_neighbours():
@@ -88,14 +98,15 @@
     return {1: me < size - 1, -1: me > 0}
 
 
-def halo(kv_ref, send_sem, recv_sem):
+def halo(kv_ref, start, per, halo_sems, chunk):
     sects, my_sect = lax.axis_size("sect"), lax.axis_index("sect")
     my_lat = lax.axis_index("lat")
     lon = kv_ref.shape[1] - 2 * WW
     exists = lat_neighbours()
     taken = {0: slice(WW, WW + lon), 1: slice(lon, WW + lon), -1: slice(WW, 2 * WW)}
     placed = {0: slice(WW, WW + lon), 1: slice(0, WW), -1: slice(WW + lon, 2 * WW + lon)}
-    landing = {0: slice(WL, 2 * WL), 1: slice(0, WL), -1: slice(2 * WL, 3 * WL)}
+    landing = {0: WL, 1: 0, -1: 2 * WL}
+    send_sem, recv_sem = halo_sems
     copies = []
     index = 0
     for dl in (1, -1, 0):
@@ -104,10 +115,10 @@
                 continue
             target = {"sect": lax.rem(my_sect + ds + sects, sects), "lat": my_lat + dl}
             copy = pltpu.make_async_remote_copy(
-                src_ref=kv_ref.at[WL : 2 * WL, taken[ds], :],
-                dst_ref=kv_ref.at[landing[dl], placed[ds], :],
-                send_sem=send_sem.at[index],
-                recv_sem=recv_sem.at[index],
+                src_ref=kv_ref.at[pl.ds(WL + start, per), taken[ds], :],
+                dst_ref=kv_ref.at[pl.ds(landing[dl] + start, per), placed[ds], :],
+                send_sem=send_sem.at[chunk, index],
+                recv_sem=recv_sem.at[chunk, index],
                 device_id=target,
                 device_id_type=MESH,
             )
@@ -117,12 +128,7 @@
                 pl.when(exists[dl])(copy.start)
             else:
                 copy.start()
-    for dl, copy in copies:
-        if dl:
-            pl.when(exists[dl])(copy.wait_send)
-            pl.when(exists[-dl])(copy.wait_recv)
-        else:
-            copy.wait()
+    return copies
 
 
 def attention(layer, shifts, scales, q_ref, kv_ref, wide, q_shifted, kv_shifted, framed, attended):
@@ -143,9 +149,8 @@
     key_row = lax.broadcasted_iota(jnp.int32, (WL * WW, WL * WW), 1) // WW
     heads = cols // HD
 
-    @pl.loop(0, frame_cols // WW)
-    def _(n):
-        at = pl.ds(pl.multiple_of(n * WW, WW), WW)
+    for n in range(frame_cols // WW):
+        at = slice(n * WW, (n + 1) * WW)
         for m in range(frame_rows // WL):
             rows = slice(m * WL, (m + 1) * WL)
             queries = q_shifted[rows, at, :].reshape(WL * WW, cols)
@@ -163,34 +168,34 @@
                 scale = scales[layer, h]
                 expo = jnp.where(usable, jnp.exp((scores - 1.0) * scale), 0.0)
                 total = jnp.sum(expo, axis=1, keepdims=True)
-                weights = (expo / total).astype(jnp.bfloat16)
-                result = jnp.where(mine, dot(weights, values), result)
+                mixed = dot(expo.astype(jnp.bfloat16), values) * (1.0 / total)
+                result = jnp.where(mine, mixed, result)
             framed[rows, at, :] = result.reshape(WL, WW, cols)
 
     for r in range(lat_rows):
         attended[r * lon : (r + 1) * lon, :] = turned(framed[WL - a + r], WW - b, lon)
 
 
-def pieces(stack_rows):
+def pieces(stack_rows, lat_first):
     sect, lat = lax.axis_index("sect"), lax.axis_index("lat")
     core, across, pair = lax.rem(sect, 2), sect // 2, lax.rem(lat, 2)
     step = stack_rows // 8
-    own = (core * 2 + across) * 2 + pair
-    ranges = [(own, 1), (core * 2 + across, 2), (core, 4)]
-    targets = [
-        {"lat": lat + 1 - 2 * pair},
-        {"sect": sect + 2 - 4 * across},
-        {"sect": sect + 1 - 2 * core},
-    ]
+    by_lat, by_chip = {"lat": lat + 1 - 2 * pair}, {"sect": sect + 2 - 4 * across}
+    by_core = {"sect": sect + 1 - 2 * core}
+    if lat_first:
+        outer, inner, targets = across, pair, [by_lat, by_chip, by_core]
+    else:
+        outer, inner, targets = pair, across, [by_chip, by_lat, by_core]
+    ranges = [((core * 2 + outer) * 2 + inner, 1), (core * 2 + outer, 2), (core, 4)]
     at = [
         pl.ds(pl.multiple_of(index * (count * step), 16), count * step) for index, count in ranges
     ]
     return at, targets
 
 
-def spread(stack, others, send_sem, recv_sem):
+def spread(stack, others, send_sem, recv_sem, lat_first):
     vars_, my_var, to_var, from_var = ring("var")
-    at, targets = pieces(stack.shape[0])
+    at, targets = pieces(stack.shape[0], lat_first)
     groups = [
         [
             pltpu.make_async_remote_copy(
@@ -260,10 +265,10 @@
 
 
 def whole_kernel(
-    patches, table, wqkv, stack, scales, params, decode, shifts, out_ref,
-    patch_in, table_in, params_in, part, part_in, full, others, attended_in,
+    patches, table, wqkv, wout, w_in, w_out, scales, gains, biases, decode, shifts, out_ref,
+    stack, patch_in, table_in, params_in, part, part_in, full, others, attended_in,
     q_ref, kv_ref, wide, q_shifted, kv_shifted, framed, attended,
-    decode_in, made, landed, send_sem, recv_sem, halo_send, halo_recv, spread_send, spread_recv,
+    decode_in, made, landed, send_sem, recv_sem, halo_send, halo_recv, spread_send, spread_recv, patch_send, patch_recv,
 ):
     sems = (send_sem, recv_sem)
     sects, my_sect, to_sect, from_sect = ring("sect")
@@ -277,6 +282,10 @@
         kv_ref[layer, :WL] = jnp.zeros_like(kv_ref[layer, :WL])
         kv_ref[layer, 2 * WL :] = jnp.zeros_like(kv_ref[layer, 2 * WL :])
     q_ref[...] = jnp.zeros_like(q_ref)
+    at = 0
+    for weight in (wout, w_in, w_out):
+        stack[:, at : at + weight.shape[1], :] = weight[...]
+        at += weight.shape[1]
     exists = lat_neighbours()
     barrier = pltpu.get_barrier_semaphore()
     my_lat = lax.axis_index("lat")
@@ -295,26 +304,55 @@
     pl.semaphore_wait(barrier, sects + vars_ - 2 + 3 * around)
 
     last = 4 + 4 * layers
-    moved, later = [], []
-    for d in range(1, sects):
-        t = to_sect[d]
-        moved.append(send(table, table_in.at[d - 1], sems, 0, d, "sect", t))
-        moved.append(
-            send(
-                patches.at[:, pl.ds(pl.multiple_of(t * cols, cols), cols), :],
-                patch_in.at[d - 1], sems, 1, d, "sect", t,
+    later = []
+    other_core = my_sect + 1 - 2 * lax.rem(my_sect, 2)
+    other_chip = lax.rem(my_sect + 2, sects)
+
+    def pass_table(source, owner, target, index):
+        slot = lax.rem(target - owner + sects, sects) - 1
+        return send(source, table_in.at[slot], sems, 0, index, "sect", target)
+
+    tables = [pass_table(table, my_sect, other_chip, 0), pass_table(table, my_sect, other_core, 1)]
+    chunks = []
+    for k in range(vars_):
+        lat = pl.ds(to_var[(k + 1) % vars_] * per, per)
+        group = []
+        for d in range(1, sects):
+            at = pl.ds(pl.multiple_of(to_sect[d] * cols, cols), cols)
+            copy = pltpu.make_async_remote_copy(
+                src_ref=patches.at[lat, at, :],
+                dst_ref=patch_in.at[d - 1, lat],
+                send_sem=patch_send.at[k, d],
+                recv_sem=patch_recv.at[k, d],
+                device_id={"sect": to_sect[d]},
+                device_id_type=MESH,
             )
-        )
-    params_in[my_var] = params[...]
+            copy.start()
+            group.append(copy)
+        chunks.append(group)
+    lines = gains.shape[0]
+    params_in[my_var, :lines] = gains[...]
+    params_in[my_var, lines:] = biases[...]
     for d in range(1, vars_):
-        later.append(send(params, params_in.at[my_var], sems, 2, d, "var", to_var[d]))
-    carried = [
-        spread(stack.at[layer], others.at[layer], spread_send.at[layer], spread_recv.at[layer])
-        for layer in range(layers)
-    ]
+        own = params_in.at[my_var]
+        later.append(send(own, own, sems, 2, d, "var", to_var[d]))
+    stack_rows = stack.shape[1]
+    half = (stack_rows // 128 + 1) // 2 * 128
+    carried = []
+    for layer in range(layers):
+        halves = [
+            spread(
+                stack.at[layer, at], others.at[layer, :, at],
+                spread_send.at[layer, k], spread_recv.at[layer, k], k == 0,
+            )
+            for k, at in enumerate((slice(0, half), slice(half, stack_rows)))
+        ]
+        carried.append([a + b for a, b in zip(*halves)])
     advance(carried[0], 0)
-    for copy in moved:
-        copy.wait()
+    tables[0].wait()
+    relayed = pass_table(table_in.at[sects // 2 - 1], other_chip, other_core, 2)
+    tables[1].wait()
+    relayed.wait()
     weights = jnp.concatenate([table[...]] + [table_in[d] for d in range(sects - 1)], axis=0)
 
     def partial_of(owner):
@@ -326,11 +364,15 @@
 
     outgoing = []
     for d in range(1, vars_):
+        for copy in chunks[d - 1]:
+            copy.wait()
         part[d - 1] = partial_of(to_var[d]).astype(jnp.bfloat16)
         outgoing.append(
             send(part.at[d - 1], part_in.at[d - 1], sems, 3, d, "var", to_var[d])
         )
     advance(carried[0], 1)
+    for copy in chunks[vars_ - 1]:
+        copy.wait()
     total = partial_of(my_var)
     for d in range(1, vars_):
         outgoing[d - 1].wait()
@@ -341,7 +383,8 @@
     advance(carried[0], 2)
     for layer in range(layers):
         gather_project(
-            full.at[layer], wqkv[layer], q_ref, kv_ref.at[layer], sems, 7 + 4 * layer
+            full.at[layer], wqkv.at[layer], q_ref, kv_ref.at[layer], sems, 7 + 4 * layer,
+            (halo_send.at[layer], halo_recv.at[layer]),
         )
         if layer == 0:
             for copy in later:
@@ -349,7 +392,6 @@
         advance(carried[layer], 3)
         if layer + 1 < layers:
             advance(carried[layer + 1], 0)
-        halo(kv_ref.at[layer], halo_send.at[layer], halo_recv.at[layer])
         attention(
             layer, shifts, scales, q_ref, kv_ref.at[layer], wide, q_shifted, kv_shifted,
             framed, attended.at[layer],
@@ -416,22 +458,21 @@
     bf = jnp.bfloat16
     vmem = pl.BlockSpec(memory_space=pltpu.VMEM)
     smem = pl.BlockSpec(memory_space=pltpu.SMEM)
-    wqkv = qkv_weight.reshape(layers, width, 3 * head_cols)
-    params = jnp.concatenate(
-        [norm_gain.reshape(2 * layers, -1), norm_bias.reshape(2 * layers, -1)], axis=0
-    )
-    stack = jnp.concatenate([out_weight, mlp_in_weight, mlp_out_weight], axis=1)
+    wqkv = qkv_weight.transpose(0, 2, 1, 3)
+    gains, biases = norm_gain.reshape(2 * layers, -1), norm_bias.reshape(2 * layers, -1)
+    stack_rows = out_weight.shape[1] + mlp_in_weight.shape[1] + mlp_out_weight.shape[1]
     shards = pltpu.VMEM((vars_ - 1, rows, width), bf)
     ext_rows, ext_cols = lat_rows + 2 * WL, cols + 2 * WW
     phases = 4 + 4 * layers + 2 + vars_
     scratch = [
+        pltpu.VMEM((layers, stack_rows, width), bf),
         pltpu.VMEM((sects - 1, lat_rows, cols, patch_dim), bf),
         pltpu.VMEM((sects - 1, patch_dim, width), bf),
-        pltpu.VMEM((vars_,) + params.shape, jnp.float32),
+        pltpu.VMEM((vars_, 4 * layers, gains.shape[1]), jnp.float32),
         shards,
         shards,
         pltpu.VMEM((layers + 1, vars_, rows, width), bf),
-        pltpu.VMEM((layers, vars_ - 1) + stack.shape[1:], bf),
+        pltpu.VMEM((layers, vars_ - 1, stack_rows, width), bf),
         pltpu.VMEM((layers, vars_ - 1, rows, head_cols), bf),
         pltpu.VMEM((ext_rows, ext_cols, head_cols), jnp.float32),
         pltpu.VMEM((layers, ext_rows, ext_cols, 2 * head_cols), bf),
@@ -445,23 +486,25 @@
         pltpu.VMEM((sects, lat_rows, cols, patch_dim), bf),
         pltpu.SemaphoreType.DMA((phases, 4)),
         pltpu.SemaphoreType.DMA((phases, 4)),
-        pltpu.SemaphoreType.DMA((layers, 8)),
-        pltpu.SemaphoreType.DMA((layers, 8)),
-        pltpu.SemaphoreType.DMA((layers, vars_ + 2)),
-        pltpu.SemaphoreType.DMA((layers, vars_ + 2)),
+        pltpu.SemaphoreType.DMA((layers, vars_, 8)),
+        pltpu.SemaphoreType.DMA((layers, vars_, 8)),
+        pltpu.SemaphoreType.DMA((layers, 2, vars_ + 2)),
+        pltpu.SemaphoreType.DMA((layers, 2, vars_ + 2)),
+        pltpu.SemaphoreType.DMA((vars_, sects)),
+        pltpu.SemaphoreType.DMA((vars_, sects)),
     ]
     out = pl.pallas_call(
         whole_kernel,
         out_shape=jax.ShapeDtypeStruct((lat_rows, lon_total, patch_dim), bf),
-        in_specs=[vmem] * 4 + [smem] + [vmem] * 2 + [smem],
+        in_specs=[vmem] * 6 + [smem] + [vmem] * 3 + [smem],
         out_specs=vmem,
         scratch_shapes=scratch,
         compiler_params=pltpu.CompilerParams(
             collective_id=0, has_side_effects=True, vmem_limit_bytes=48 * 1024 * 1024
         ),
     )(
-        patches[0], embed_weight[0], wqkv, stack,
-        logit_scale, params, decode_weight[0], shifts,
+        patches[0], embed_weight[0], wqkv, out_weight, mlp_in_weight, mlp_out_weight,
+        logit_scale, gains, biases, decode_weight[0], shifts,
     )
     return out[None]
 

time: 150 us -> 130 us (0.87)
  Pallas kernels: 145 us -> 120 us
  local copies, waits for them, and re-layouts: 2.59 us -> 8.9 us
  other arithmetic: 2.25 us -> 0 us
    pallas_call x1, Pallas kernels: 145 us -> 120 us  [per_device(): pl.pallas_call(whole_kernel, out_shape=jax.ShapeDtypeStruct((lat_rows, lo...]
    unnamed x16 -> x23, local copies, waits for them, and re-layouts: 2.24 us -> 8.9 us
    concatenate x2 -> x0, other arithmetic: 2.25 us -> none  [the longest x1 1.44 us: per_device(): stack = jnp.concatenate([out_weight, mlp_in_weight, mlp_out_weight], axis=1)]
where the time goes in v4:
time: 130 us; the launch traced here: 129 us
  Pallas kernels  120 us (92%)
  local copies, waits for them, and re-layouts  8.9 us (7%)
    pallas_call x1, Pallas kernels, per_device(): pl.pallas_call(whole_kernel, out_shape=jax.ShapeDtypeStruct((lat_rows, lo...  120 us
    unnamed x23, local copies, waits for them, and re-layouts  8.9 us

profile of v4, /device:TPU:0, one launch (start us, length us, event | category | flops | bytes accessed | tf_op | source)
XLA Modules:
  0.0 129.2 jit_solution(11562342062818045193)
XLA Ops:
  0.0 0.0 copy-start.10
  0.0 0.0 copy-start.8
  0.0 0.0 copy-start.7
  0.0 0.0 copy-start.9
  0.0 0.7 copy-done.10
  0.7 0.0 copy-done.8
  0.7 0.0 copy-done.7
  0.7 0.0 copy-done.9
  0.7 0.0 copy-start
  0.7 1.2 copy-done
  2.0 0.0 copy-start.1
  2.0 1.2 copy-done.1
  3.2 0.0 copy-start.2
  3.2 1.1 copy-done.2
  4.3 0.0 copy-start.3
  4.3 1.0 copy-done.3
  5.4 0.0 copy-start.4
  5.4 0.9 copy-done.4
  6.3 0.0 copy-start.5
  6.3 0.9 copy-done.5
  7.2 0.0 copy-start.6
  7.2 0.9 copy-done.6
  8.1 120.2 %shard_map.109 = bf16[8,256,128]{2,1,0:T(8,128)(2,1)S(1)} custom-call(bf16[8,256,128]{2,1,0:T(8,128)(2,1)S(1)} %bitcast.9, bf16[128,512]{1,0:T(8,128)(2,1)S(1)} %bitcast.10, bf16[2,3,512,128]{3,2,1,0:T(8,128)(2,1)S(1)} %bitcast.8, bf16[2,128,512]{2,1,0:T(8,128)(2,1)S(1)} %copy-done.4, bf16[2,512,512]{2,1,0:T(8,128)(2,1)S(1)} %copy-done, ...), custom_call_target="tpu_custom_call" | custom-call | tf_op jit(solution)/shard_map/pallas_call | solution.py:496
  128.4 0.8 copy.13
Async XLA Ops:
  0.0 0.7 copy-start.10
  0.0 0.7 copy-start.8
  0.0 0.7 copy-start.7
  0.0 0.7 copy-start.9
  0.7 1.2 copy-start
  2.0 1.2 copy-start.1
  3.2 1.1 copy-start.2
  4.3 1.0 copy-start.3
  5.4 0.9 copy-start.4
  6.3 0.9 copy-start.5
  7.2 0.9 copy-start.6

commit v5 on v4

--- a/solution.py
+++ b/solution.py
@@ -131,7 +131,9 @@
     return copies
 
 
-def attention(layer, shifts, scales, q_ref, kv_ref, wide, q_shifted, kv_shifted, framed, attended):
+def attention(
+    layer, shifts, scales, q_ref, kv_ref, wide, q_shifted, kv_shifted, framed, attended, between
+):
     lat_rows, lon = WL, q_ref.shape[1] - 2 * WW
     cols = q_ref.shape[2]
     a, b = shifts[layer, 0], shifts[layer, 1]
@@ -145,32 +147,39 @@
     for r in range(frame_rows):
         kv_shifted[r] = turned(wide[a + r], b, frame_cols)
         q_shifted[r] = turned(q_ref[a + r], b, frame_cols)
-    lane = lax.broadcasted_iota(jnp.int32, (WL * WW, cols), 1)
-    key_row = lax.broadcasted_iota(jnp.int32, (WL * WW, WL * WW), 1) // WW
-    heads = cols // HD
+    heads, window = cols // HD, WL * WW
+    lane = lax.broadcasted_iota(jnp.int32, (window, cols), 1)
+    key_row = lax.broadcasted_iota(jnp.int32, (heads * window, window), 1) // WW
+    head_row = lax.broadcasted_iota(jnp.int32, (heads * window, window), 0) // window
+    scale = jnp.zeros((heads * window, window), jnp.float32)
+    for h in range(heads):
+        scale = jnp.where(head_row == h, scales[layer, h], scale)
+    masks = [(lane >= h * HD) & (lane < (h + 1) * HD) for h in range(heads)]
 
     for n in range(frame_cols // WW):
         at = slice(n * WW, (n + 1) * WW)
         for m in range(frame_rows // WL):
             rows = slice(m * WL, (m + 1) * WL)
-            queries = q_shifted[rows, at, :].reshape(WL * WW, cols)
-            paired = kv_shifted[rows, at, :].reshape(WL * WW, 2 * cols)
+            queries = q_shifted[rows, at, :].reshape(window, cols)
+            paired = kv_shifted[rows, at, :].reshape(window, 2 * cols)
             keys, values = paired[:, :cols], paired[:, cols:]
             place = my_lat * lat_rows - WL + a + m * WL + key_row
             usable = (place >= 0) & (place < lats * lat_rows)
-            result = jnp.zeros((WL * WW, cols), jnp.float32)
-            for h in range(heads):
-                mine = (lane >= h * HD) & (lane < (h + 1) * HD)
-                part = jnp.where(mine, queries, jnp.zeros_like(queries))
-                scores = lax.dot_general(
-                    part, keys, (((1,), (1,)), ((), ())), preferred_element_type=jnp.float32
-                )
-                scale = scales[layer, h]
-                expo = jnp.where(usable, jnp.exp((scores - 1.0) * scale), 0.0)
-                total = jnp.sum(expo, axis=1, keepdims=True)
-                mixed = dot(expo.astype(jnp.bfloat16), values) * (1.0 / total)
-                result = jnp.where(mine, mixed, result)
+            split = jnp.concatenate(
+                [jnp.where(mine, queries, jnp.zeros_like(queries)) for mine in masks], axis=0
+            )
+            scores = lax.dot_general(
+                split, keys, (((1,), (1,)), ((), ())), preferred_element_type=jnp.float32
+            )
+            expo = jnp.where(usable, jnp.exp((scores - 1.0) * scale), 0.0)
+            total = jnp.sum(expo, axis=1, keepdims=True)
+            mixed = dot(expo.astype(jnp.bfloat16), values) * (1.0 / total)
+            result = jnp.zeros((window, cols), jnp.float32)
+            for h, mine in enumerate(masks):
+                result = jnp.where(mine, mixed[h * window : (h + 1) * window], result)
             framed[rows, at, :] = result.reshape(WL, WW, cols)
+        for step in between.get(n, ()):
+            advance(*step)
 
     for r in range(lat_rows):
         attended[r * lon : (r + 1) * lon, :] = turned(framed[WL - a + r], WW - b, lon)
@@ -234,7 +243,7 @@
             copy.start()
 
 
-def feed(layer, attended, attended_in, stack, others, params, x_ref, out_ref, sems, phase):
+def feed(layer, attended, attended_in, stack, others, params, x_ref, out_ref, sems, phase, steps):
     vars_, my_var, to_var, from_var = ring("var")
     rows, heads_part = attended_in.shape[1:]
     width = x_ref.shape[2]
@@ -249,23 +258,33 @@
         outgoing.append(
             send(attended.at[at], attended_in.at[d - 1], sems, phase, d, "var", to_var[d])
         )
+    for step in steps[0]:
+        advance(*step)
     own = attended[pl.ds(pl.multiple_of(my_var * rows, rows), rows), :]
     total = dot(own, stack[:heads_part])
     for d in range(1, vars_):
         outgoing[d - 1].wait()
         total = total + dot(attended_in[d - 1], others[d - 1, :heads_part])
+    for step in steps[1]:
+        advance(*step)
     mid = norm_add(x_ref[my_var], total, chosen(0, 0), chosen(1, 0))
     first = slice(heads_part, heads_part + width)
+    shards = [stack] + [others.at[d] for d in range(vars_ - 1)]
+    hidden = [
+        jax.nn.gelu(dot(mid, shard[first]), approximate=True).astype(jnp.bfloat16)
+        for shard in shards
+    ]
+    for step in steps[2]:
+        advance(*step)
     total = jnp.zeros((rows, width), jnp.float32)
-    for d in range(vars_):
-        shard = stack if d == 0 else others.at[d - 1]
-        hidden = jax.nn.gelu(dot(mid, shard[first]), approximate=True).astype(jnp.bfloat16)
-        total = total + dot(hidden, shard[heads_part + width :])
+    for part, shard in zip(hidden, shards):
+        total = total + dot(part, shard[heads_part + width :])
     out_ref[my_var] = norm_add(mid, total, chosen(0, 1), chosen(1, 1))
 
 
 def whole_kernel(
-    patches, table, wqkv, wout, w_in, w_out, scales, gains, biases, decode, shifts, out_ref,
+    patches, table_hbm, wqkv_hbm, wout, w_in, w_out, scales, gains, biases, decode_hbm, shifts, out_ref,
+    own_patch, table, wqkv, decode, load_sem,
     stack, patch_in, table_in, params_in, part, part_in, full, others, attended_in,
     q_ref, kv_ref, wide, q_shifted, kv_shifted, framed, attended,
     decode_in, made, landed, send_sem, recv_sem, halo_send, halo_recv, spread_send, spread_recv, patch_send, patch_recv,
@@ -282,10 +301,20 @@
         kv_ref[layer, :WL] = jnp.zeros_like(kv_ref[layer, :WL])
         kv_ref[layer, 2 * WL :] = jnp.zeros_like(kv_ref[layer, 2 * WL :])
     q_ref[...] = jnp.zeros_like(q_ref)
+    own_cols = pl.ds(pl.multiple_of(my_sect * cols, cols), cols)
+    pairs = []
     at = 0
     for weight in (wout, w_in, w_out):
-        stack[:, at : at + weight.shape[1], :] = weight[...]
+        pairs.append((weight, stack.at[:, at : at + weight.shape[1], :]))
         at += weight.shape[1]
+    pairs += [
+        (table_hbm, table), (patches.at[:, own_cols, :], own_patch), (wqkv_hbm, wqkv),
+        (decode_hbm, decode),
+    ]
+    loads = []
+    for index, (source, target) in enumerate(pairs):
+        loads.append(pltpu.make_async_copy(source, target, load_sem.at[index]))
+        loads[-1].start()
     exists = lat_neighbours()
     barrier = pltpu.get_barrier_semaphore()
     my_lat = lax.axis_index("lat")
@@ -312,7 +341,7 @@
         slot = lax.rem(target - owner + sects, sects) - 1
         return send(source, table_in.at[slot], sems, 0, index, "sect", target)
 
-    tables = [pass_table(table, my_sect, other_chip, 0), pass_table(table, my_sect, other_core, 1)]
+    tables = [pass_table(table_hbm, my_sect, other_chip, 0), pass_table(table_hbm, my_sect, other_core, 1)]
     chunks = []
     for k in range(vars_):
         lat = pl.ds(to_var[(k + 1) % vars_] * per, per)
@@ -337,7 +366,7 @@
         own = params_in.at[my_var]
         later.append(send(own, own, sems, 2, d, "var", to_var[d]))
     stack_rows = stack.shape[1]
-    half = (stack_rows // 128 + 1) // 2 * 128
+    half = stack_rows - w_out.shape[1]
     carried = []
     for layer in range(layers):
         halves = [
@@ -347,17 +376,21 @@
             )
             for k, at in enumerate((slice(0, half), slice(half, stack_rows)))
         ]
-        carried.append([a + b for a, b in zip(*halves)])
-    advance(carried[0], 0)
+        carried.append(halves)
+    for load in loads[:3]:
+        load.wait()
+    advance(carried[0][0], 0)
     tables[0].wait()
     relayed = pass_table(table_in.at[sects // 2 - 1], other_chip, other_core, 2)
+    for load in loads[3:]:
+        load.wait()
     tables[1].wait()
     relayed.wait()
     weights = jnp.concatenate([table[...]] + [table_in[d] for d in range(sects - 1)], axis=0)
 
     def partial_of(owner):
         lat = pl.ds(owner * per, per)
-        own = patches[lat, pl.ds(pl.multiple_of(my_sect * cols, cols), cols), :]
+        own = own_patch[lat]
         blocks = [own] + [patch_in[d, lat] for d in range(sects - 1)]
         x = jnp.concatenate([block.reshape(rows, depth) for block in blocks], axis=1)
         return dot(x, weights)
@@ -370,7 +403,7 @@
         outgoing.append(
             send(part.at[d - 1], part_in.at[d - 1], sems, 3, d, "var", to_var[d])
         )
-    advance(carried[0], 1)
+    advance(carried[0][0], 1)
     for copy in chunks[vars_ - 1]:
         copy.wait()
     total = partial_of(my_var)
@@ -380,7 +413,7 @@
     full[0, my_var] = total.astype(jnp.bfloat16)
     for d in range(1, sects):
         later.append(send(decode, decode_in.at[d - 1], sems, last, d, "sect", to_sect[d]))
-    advance(carried[0], 2)
+    advance(carried[0][0], 2)
     for layer in range(layers):
         gather_project(
             full.at[layer], wqkv.at[layer], q_ref, kv_ref.at[layer], sems, 7 + 4 * layer,
@@ -389,22 +422,32 @@
         if layer == 0:
             for copy in later:
                 copy.wait()
-        advance(carried[layer], 3)
-        if layer + 1 < layers:
-            advance(carried[layer + 1], 0)
+        early, late = carried[layer]
+        ahead = carried[layer + 1] if layer + 1 < layers else None
+        advance(early, 3)
+        if layer == 0:
+            advance(late, 0)
+            between = {1: [(late, 1)], 3: [(late, 2)]}
+        else:
+            advance(late, 1)
+            between = {1: [(late, 2)]}
+        if ahead:
+            advance(ahead[0], 0)
         attention(
             layer, shifts, scales, q_ref, kv_ref.at[layer], wide, q_shifted, kv_shifted,
-            framed, attended.at[layer],
+            framed, attended.at[layer], between,
         )
-        advance(carried[layer], 4)
-        if layer + 1 < layers:
-            advance(carried[layer + 1], 1)
         feed(
             layer, attended.at[layer], attended_in.at[layer], stack.at[layer], others.at[layer],
             params_in, full.at[layer], full.at[layer + 1], sems, 4 + 4 * layer,
+            (
+                [(early, 4)] + ([(ahead[0], 1)] if ahead else []),
+                [(late, 3)] + ([(ahead[1], 0)] if ahead else []),
+                [(late, 4)],
+            ),
         )
-        if layer + 1 < layers:
-            advance(carried[layer + 1], 2)
+        if ahead:
+            advance(ahead[0], 2)
     stream = full.at[layers]
     outgoing = [
         send(stream.at[my_var], stream.at[my_var], sems, last + 1, d, "var", to_var[d])
@@ -458,6 +501,7 @@
     bf = jnp.bfloat16
     vmem = pl.BlockSpec(memory_space=pltpu.VMEM)
     smem = pl.BlockSpec(memory_space=pltpu.SMEM)
+    hbm = pl.BlockSpec(memory_space=pltpu.HBM)
     wqkv = qkv_weight.transpose(0, 2, 1, 3)
     gains, biases = norm_gain.reshape(2 * layers, -1), norm_bias.reshape(2 * layers, -1)
     stack_rows = out_weight.shape[1] + mlp_in_weight.shape[1] + mlp_out_weight.shape[1]
@@ -465,6 +509,11 @@
     ext_rows, ext_cols = lat_rows + 2 * WL, cols + 2 * WW
     phases = 4 + 4 * layers + 2 + vars_
     scratch = [
+        pltpu.VMEM((lat_rows, cols, patch_dim), bf),
+        pltpu.VMEM((patch_dim, width), bf),
+        pltpu.VMEM((layers, 3, width, head_cols), bf),
+        pltpu.VMEM((width, patch_dim), bf),
+        pltpu.SemaphoreType.DMA((8,)),
         pltpu.VMEM((layers, stack_rows, width), bf),
         pltpu.VMEM((sects - 1, lat_rows, cols, patch_dim), bf),
         pltpu.VMEM((sects - 1, patch_dim, width), bf),
@@ -496,7 +545,7 @@
     out = pl.pallas_call(
         whole_kernel,
         out_shape=jax.ShapeDtypeStruct((lat_rows, lon_total, patch_dim), bf),
-        in_specs=[vmem] * 6 + [smem] + [vmem] * 3 + [smem],
+        in_specs=[hbm] * 6 + [smem, vmem, vmem, hbm, smem],
         out_specs=vmem,
         scratch_shapes=scratch,
         compiler_params=pltpu.CompilerParams(

time: 130 us -> 142 us (1.092)
  Pallas kernels: 120 us -> 132 us
    pallas_call x1, Pallas kernels: 120 us -> 132 us  [per_device(): pl.pallas_call(whole_kernel, out_shape=jax.ShapeDtypeStruct((lat_rows, lo...]
where the time goes in v5:
time: 142 us; the launch traced here: 141 us
  Pallas kernels  132 us (93%)
  local copies, waits for them, and re-layouts  8.9 us (6%)
    pallas_call x1, Pallas kernels, per_device(): pl.pallas_call(whole_kernel, out_shape=jax.ShapeDtypeStruct((lat_rows, lo...  132 us
    unnamed x23, local copies, waits for them, and re-layouts  8.9 us

profile of v5, /device:TPU:0, one launch (start us, length us, event | category | flops | bytes accessed | tf_op | source)
XLA Modules:
  0.0 141.4 jit_solution(9057402875940356162)
XLA Ops:
  0.0 0.0 copy-start.10
  0.0 0.0 copy-start.8
  0.0 0.0 copy-start.7
  0.0 0.0 copy-start.9
  0.0 0.7 copy-done.10
  0.7 0.0 copy-done.8
  0.7 0.0 copy-done.7
  0.7 0.0 copy-done.9
  0.7 0.0 copy-start
  0.7 1.2 copy-done
  2.0 0.0 copy-start.1
  2.0 1.2 copy-done.1
  3.2 0.0 copy-start.2
  3.2 1.1 copy-done.2
  4.3 0.0 copy-start.3
  4.3 1.0 copy-done.3
  5.4 0.0 copy-start.4
  5.4 0.9 copy-done.4
  6.3 0.0 copy-start.5
  6.3 0.9 copy-done.5
  7.2 0.0 copy-start.6
  7.2 0.9 copy-done.6
  8.1 132.5 %shard_map.109 = bf16[8,256,128]{2,1,0:T(8,128)(2,1)S(1)} custom-call(bf16[8,256,128]{2,1,0:T(8,128)(2,1)S(1)} %bitcast.9, bf16[128,512]{1,0:T(8,128)(2,1)S(1)} %bitcast.10, bf16[2,3,512,128]{3,2,1,0:T(8,128)(2,1)S(1)} %bitcast.8, bf16[2,128,512]{2,1,0:T(8,128)(2,1)S(1)} %copy-done.4, bf16[2,512,512]{2,1,0:T(8,128)(2,1)S(1)} %copy-done, ...), custom_call_target="tpu_custom_call" | custom-call | tf_op jit(solution)/shard_map/pallas_call | solution.py:545
  140.6 0.8 copy.13
Async XLA Ops:
  0.0 0.7 copy-start.10
  0.0 0.7 copy-start.8
  0.0 0.7 copy-start.7
  0.0 0.7 copy-start.9
  0.7 1.2 copy-start
  2.0 1.2 copy-start.1
  3.2 1.1 copy-start.2
  4.3 1.0 copy-start.3
  5.4 0.9 copy-start.4
  6.3 0.9 copy-start.5
  7.2 0.9 copy-start.6

commit v6 on v5

--- a/solution.py
+++ b/solution.py
@@ -132,7 +132,7 @@
 
 
 def attention(
-    layer, shifts, scales, q_ref, kv_ref, wide, q_shifted, kv_shifted, framed, attended, between
+    layer, shifts, scales, q_ref, kv_ref, wide, q_shifted, kv_shifted, framed, attended
 ):
     lat_rows, lon = WL, q_ref.shape[1] - 2 * WW
     cols = q_ref.shape[2]
@@ -178,8 +178,6 @@
             for h, mine in enumerate(masks):
                 result = jnp.where(mine, mixed[h * window : (h + 1) * window], result)
             framed[rows, at, :] = result.reshape(WL, WW, cols)
-        for step in between.get(n, ()):
-            advance(*step)
 
     for r in range(lat_rows):
         attended[r * lon : (r + 1) * lon, :] = turned(framed[WL - a + r], WW - b, lon)
@@ -379,7 +377,8 @@
         carried.append(halves)
     for load in loads[:3]:
         load.wait()
-    advance(carried[0][0], 0)
+    for half_gather in carried[0]:
+        advance(half_gather, 0)
     tables[0].wait()
     relayed = pass_table(table_in.at[sects // 2 - 1], other_chip, other_core, 2)
     for load in loads[3:]:
@@ -403,7 +402,8 @@
         outgoing.append(
             send(part.at[d - 1], part_in.at[d - 1], sems, 3, d, "var", to_var[d])
         )
-    advance(carried[0][0], 1)
+    for half_gather in carried[0]:
+        advance(half_gather, 1)
     for copy in chunks[vars_ - 1]:
         copy.wait()
     total = partial_of(my_var)
@@ -413,7 +413,8 @@
     full[0, my_var] = total.astype(jnp.bfloat16)
     for d in range(1, sects):
         later.append(send(decode, decode_in.at[d - 1], sems, last, d, "sect", to_sect[d]))
-    advance(carried[0][0], 2)
+    for half_gather in carried[0]:
+        advance(half_gather, 2)
     for layer in range(layers):
         gather_project(
             full.at[layer], wqkv.at[layer], q_ref, kv_ref.at[layer], sems, 7 + 4 * layer,
@@ -423,31 +424,22 @@
             for copy in later:
                 copy.wait()
         early, late = carried[layer]
-        ahead = carried[layer + 1] if layer + 1 < layers else None
+        ahead = carried[layer + 1] if layer + 1 < layers else []
         advance(early, 3)
-        if layer == 0:
-            advance(late, 0)
-            between = {1: [(late, 1)], 3: [(late, 2)]}
-        else:
-            advance(late, 1)
-            between = {1: [(late, 2)]}
-        if ahead:
-            advance(ahead[0], 0)
+        advance(late, 3)
+        for half_gather in ahead:
+            advance(half_gather, 0)
         attention(
             layer, shifts, scales, q_ref, kv_ref.at[layer], wide, q_shifted, kv_shifted,
-            framed, attended.at[layer], between,
+            framed, attended.at[layer],
         )
         feed(
             layer, attended.at[layer], attended_in.at[layer], stack.at[layer], others.at[layer],
             params_in, full.at[layer], full.at[layer + 1], sems, 4 + 4 * layer,
-            (
-                [(early, 4)] + ([(ahead[0], 1)] if ahead else []),
-                [(late, 3)] + ([(ahead[1], 0)] if ahead else []),
-                [(late, 4)],
-            ),
+            ([(early, 4)], [(half_gather, 1) for half_gather in ahead], [(late, 4)]),
         )
-        if ahead:
-            advance(ahead[0], 2)
+        for half_gather in ahead:
+            advance(half_gather, 2)
     stream = full.at[layers]
     outgoing = [
         send(stream.at[my_var], stream.at[my_var], sems, last + 1, d, "var", to_var[d])
@@ -549,7 +541,7 @@
         out_specs=vmem,
         scratch_shapes=scratch,
         compiler_params=pltpu.CompilerParams(
-            collective_id=0, has_side_effects=True, vmem_limit_bytes=48 * 1024 * 1024
+            collective_id=0, has_side_effects=True, vmem_limit_bytes=64 * 1024 * 1024 - 65536
         ),
     )(
         patches[0], embed_weight[0], wqkv, out_weight, mlp_in_weight, mlp_out_weight,

time: 142 us -> 124 us (0.87)
  Pallas kernels: 132 us -> 122 us
  local copies, waits for them, and re-layouts: 8.9 us -> 1.87 us
    pallas_call x1, Pallas kernels: 132 us -> 122 us  [per_device(): pl.pallas_call(whole_kernel, out_shape=jax.ShapeDtypeStruct((lat_rows, lo...]
    unnamed x23 -> x1, local copies, waits for them, and re-layouts: 8.9 us -> 1.87 us
where the time goes in v6:
time: 124 us
  Pallas kernels  122 us (98%)
  local copies, waits for them, and re-layouts  1.87 us (2%)
    pallas_call x1, Pallas kernels, per_device(): pl.pallas_call(whole_kernel, out_shape=jax.ShapeDtypeStruct((lat_rows, lo...  122 us

profile of v6, /device:TPU:0, one launch (start us, length us, event | category | flops | bytes accessed | tf_op | source)
XLA Modules:
  0.0 124.2 jit_solution(1262509496014355231)
XLA Ops:
  0.0 122.3 %shard_map.109 = bf16[8,256,128]{2,1,0:T(8,128)(2,1)} custom-call(bf16[8,256,128]{2,1,0:T(8,128)(2,1)} %bitcast.9, bf16[128,512]{1,0:T(8,128)(2,1)} %bitcast.10, bf16[2,3,512,128]{3,2,1,0:T(8,128)(2,1)} %bitcast.8, bf16[2,128,512]{2,1,0:T(8,128)(2,1)} %wout.1, bf16[2,512,512]{2,1,0:T(8,128)(2,1)} %w_in.1, bf16[2,512,512]{2,1,0:T(8,128)(2,1)} %w_out.1, ...), custom_call_target="tpu_custom_call" | custom-call | tf_op jit(solution)/shard_map/pallas_call | solution.py:537
  122.3 1.9 %copy.13 = bf16[1,8,256,128]{3,2,1,0:T(8,128)(2,1)} copy(bf16[1,8,256,128]{3,2,1,0:T(8,128)(2,1)} %bitcast.7) | data formatting | bytes 1048576

commit v7 on v6

--- a/solution.py
+++ b/solution.py
@@ -377,8 +377,7 @@
         carried.append(halves)
     for load in loads[:3]:
         load.wait()
-    for half_gather in carried[0]:
-        advance(half_gather, 0)
+    advance(carried[0][0], 0)
     tables[0].wait()
     relayed = pass_table(table_in.at[sects // 2 - 1], other_chip, other_core, 2)
     for load in loads[3:]:
@@ -402,8 +401,8 @@
         outgoing.append(
             send(part.at[d - 1], part_in.at[d - 1], sems, 3, d, "var", to_var[d])
         )
-    for half_gather in carried[0]:
-        advance(half_gather, 1)
+    advance(carried[0][0], 1)
+    advance(carried[0][1], 0)
     for copy in chunks[vars_ - 1]:
         copy.wait()
     total = partial_of(my_var)
@@ -413,8 +412,8 @@
     full[0, my_var] = total.astype(jnp.bfloat16)
     for d in range(1, sects):
         later.append(send(decode, decode_in.at[d - 1], sems, last, d, "sect", to_sect[d]))
-    for half_gather in carried[0]:
-        advance(half_gather, 2)
+    advance(carried[0][0], 2)
+    advance(carried[0][1], 1)
     for layer in range(layers):
         gather_project(
             full.at[layer], wqkv.at[layer], q_ref, kv_ref.at[layer], sems, 7 + 4 * layer,
@@ -426,7 +425,7 @@
         early, late = carried[layer]
         ahead = carried[layer + 1] if layer + 1 < layers else []
         advance(early, 3)
-        advance(late, 3)
+        advance(late, 3 if layer else 2)
         for half_gather in ahead:
             advance(half_gather, 0)
         attention(
@@ -436,7 +435,7 @@
         feed(
             layer, attended.at[layer], attended_in.at[layer], stack.at[layer], others.at[layer],
             params_in, full.at[layer], full.at[layer + 1], sems, 4 + 4 * layer,
-            ([(early, 4)], [(half_gather, 1) for half_gather in ahead], [(late, 4)]),
+            ([(early, 4)], [(half_gather, 1) for half_gather in ahead] + ([] if layer else [(late, 3)]), [(late, 4)]),
         )
         for half_gather in ahead:
             advance(half_gather, 2)

time: 124 us -> 124 us (level)
  no operation moved by 1% of the time
where the time goes in v7:
time: 124 us
  Pallas kernels  122 us (98%)
  local copies, waits for them, and re-layouts  1.87 us (2%)
    pallas_call x1, Pallas kernels, per_device(): pl.pallas_call(whole_kernel, out_shape=jax.ShapeDtypeStruct((lat_rows, lo...  122 us

profile of v7, /device:TPU:0, one launch (start us, length us, event | category | flops | bytes accessed | tf_op | source)
XLA Modules:
  0.0 124.3 jit_solution(13381704210139601067)
XLA Ops:
  0.0 122.4 %shard_map.109 = bf16[8,256,128]{2,1,0:T(8,128)(2,1)} custom-call(bf16[8,256,128]{2,1,0:T(8,128)(2,1)} %bitcast.9, bf16[128,512]{1,0:T(8,128)(2,1)} %bitcast.10, bf16[2,3,512,128]{3,2,1,0:T(8,128)(2,1)} %bitcast.8, bf16[2,128,512]{2,1,0:T(8,128)(2,1)} %wout.1, bf16[2,512,512]{2,1,0:T(8,128)(2,1)} %w_in.1, bf16[2,512,512]{2,1,0:T(8,128)(2,1)} %w_out.1, ...), custom_call_target="tpu_custom_call" | custom-call | tf_op jit(solution)/shard_map/pallas_call | solution.py:536
  122.4 1.9 %copy.13 = bf16[1,8,256,128]{3,2,1,0:T(8,128)(2,1)} copy(bf16[1,8,256,128]{3,2,1,0:T(8,128)(2,1)} %bitcast.7) | data formatting | bytes 1048576
